TPU v7x, 32 devices: a whole 2x2x4 slice. The times are simulated.
32 devices in a mesh: tm: 8 (over z, x), space: 4 (over y, core).
Axes of the slice: x: 2, y: 2, z: 4, core: 2. Of those that a mesh axis runs over, the one named last changes fastest.
Arguments:
- guess: float32 [8, 1024, 1024], P('tm', 'space'), may hold values from -2.5 to 2.5
- kappa: float32 [1024, 1024], P('space'), may hold values from 0.25 to 1
- rate: float32 [1024, 1024], P('space'), may hold values from 0.005 to 0.02
Outputs:
- c_points: float32 [8, 1024, 1024], P('tm', 'space')
- last_fine: float32 [8, 1024, 1024], P('tm', 'space')
All inputs are finite; a program needn't handle non-finite values.
Results may differ from a plain program's by a relative error of at most 0.00002.
Values sent between devices are 32-bit elements; how exact they have to be, the bound alone decides.
A program may use at most 64 MiB of HBM per device.

v0:
```python
import jax
import jax.numpy as jnp
from jax import lax
from jax.sharding import PartitionSpec as P

STEPS = 4
GROUP = 4
SWEEPS = 2


DIFFUSION = 0.05


def extended(shard, sides, width):
    for axis, dim in sides:
        peers, length = (lax.axis_size(axis), shard.shape[dim])
        up = [(i, (i + 1) % peers) for i in range(peers - 1)]
        down = [(j, i) for i, j in up]
        last = lax.slice_in_dim(shard, length - width, length, axis=dim)
        initial = lax.slice_in_dim(shard, 0, width, axis=dim)
        before = lax.ppermute(last, axis, up)
        after = lax.ppermute(initial, axis, down)
        shard = jnp.concatenate([before, shard, after], axis=dim)
    return shard


def from_behind(value, axis, steps):
    count = lax.axis_size(axis)
    initial, last = (max(0, -steps), min(count, count - steps))
    return lax.ppermute(value, axis, [(source, source + steps) for source in range(initial, last)])


def advance_padded(padded, kappa, rate, scale):
    centre = padded[1:-1, 1:-1]
    laplace = (
        padded[2:, 1:-1] + padded[:-2, 1:-1] + padded[1:-1, 2:] + padded[1:-1, :-2] - 4.0 * centre
    )
    return centre + scale * (
        DIFFUSION * kappa * laplace + rate * (centre - centre * centre * centre)
    )


def deep_border(state, count):
    return extended(state, (("space", 0),), count)


def deep_step(wide, margin, widened, scale):
    rows = widened.shape[1] - 2 * STEPS
    height = wide.shape[0] - 2
    lower = STEPS - (margin - 1)
    kappa_rows = widened[0, lower : lower + height]
    rate_rows = widened[1, lower : lower + height]
    stepped = advance_padded(jnp.pad(wide, ((0, 0), (1, 1))), kappa_rows, rate_rows, scale)
    strip = lax.axis_index("space")
    total = rows * lax.axis_size("space")
    global_rows = strip * rows - (margin - 1) + lax.broadcasted_iota(jnp.int32, stepped.shape, 0)
    inside = (global_rows >= 0) & (global_rows < total)
    return jnp.where(inside, stepped, jnp.zeros_like(stepped))


def deep_march(wide, margin, widened, count):
    for repeat in range(count):
        wide = deep_step(wide, margin, widened, 1.0)
        margin = margin - 1
    return wide


def forward(state):
    return from_behind(state, "tm", 1)


def local(guess, kappa, rate):
    position = lax.axis_index("tm")
    member = position % GROUP
    coarse_scale = float(STEPS)
    state = guess[0]
    incoming = forward(state)
    widened = extended(jnp.stack([kappa, rate]), (("space", 1),), STEPS)
    marched = deep_march(deep_border(incoming, STEPS), STEPS, widened, STEPS)
    relaxed = jnp.where(position == 0, state, marched)
    incoming = forward(relaxed)
    wide = deep_border(incoming, STEPS)
    rows = relaxed.shape[0]
    band = jnp.pad(wide[STEPS - 1 : STEPS + rows + 1], ((0, 0), (1, 1)))
    coarse_image = advance_padded(band, kappa, rate, coarse_scale)
    fine_image = deep_march(wide, STEPS, widened, STEPS)
    defect = jnp.where(position == 0, jnp.zeros_like(fine_image), fine_image - coarse_image)
    coarse = relaxed
    for sweep_number in range(SWEEPS):
        for turn in range(GROUP):
            arrived = from_behind(coarse, "tm", 1)
            framed = extended(arrived, (("space", 0),), 1)
            framed = jnp.pad(framed, ((0, 0), (1, 1)))
            updated = advance_padded(framed, kappa, rate, coarse_scale) + defect
            if turn + 1 < GROUP:
                active = member == turn + 1
            else:
                active = (member == 0) & (position >= GROUP)
            coarse = jnp.where(active, updated, coarse)
    last_fine = deep_march(deep_border(coarse, STEPS - 1), STEPS - 1, widened, STEPS - 1)
    return (coarse[None], last_fine[None])


def solution(mesh):
    return jax.shard_map(
        local,
        mesh=mesh,
        in_specs=(P("tm", "space", None), P("space", None), P("space", None)),
        out_specs=(P("tm", "space", None), P("tm", "space", None)),
        check_vma=False,
    )
```

profile of v0, /device:TPU:27, one launch (start us, length us, event | category | flops | bytes accessed | tf_op | source)
XLA Modules:
  0.0 365.1 jit_solution(16139672697450203209)
XLA Ops:
  2.9 3.7 %collective-permute-start.3 = (f32[2,4,1024]{2,1,0:T(4,128)S(1)}, f32[2,4,1024]{2,1,0:T(4,128)S(1)}, u32[]{:S(2)}, u32[]{:S(2)}) collective-permute-start(f32[2,4,1024]{2,1,0:T(4,128)S(1)} %get-tuple-element.4), channel_id=1, source_target_pairs={{0,1},{1,2},{2,3},{4,5},{5,6},{6,7},{8,9},{9,10},{10,11},{12,13},{... | collective-permute-start | bytes 98312 | tf_op jit(solution)/shard_map/ppermute | solution.py:21
  8.6 18.2 %collective-permute-done = f32[256,1024]{1,0:T(8,128)S(1)} collective-permute-done((f32[256,1024]{1,0:T(8,128)}, f32[256,1024]{1,0:T(8,128)S(1)}, u32[]{:S(2)}, u32[]{:S(2)}) %collective-permute-start) | collective-permute-done | bytes 1048608 | tf_op jit(solution)/shard_map/ppermute | solution.py:30
  26.8 4.6 %collective-permute-start.1 = (f32[4,1024]{1,0:T(4,128)S(1)}, f32[4,1024]{1,0:T(4,128)S(1)}, u32[]{:S(2)}, u32[]{:S(2)}) collective-permute-start(f32[4,1024]{1,0:T(4,128)S(1)} %get-tuple-element.26), channel_id=1, source_target_pairs={{0,1},{1,2},{2,3},{4,5},{5,6},{6,7},{8,9},{9,10},{10,11},{12,13},{... | collective-permute-start | bytes 49160 | tf_op jit(solution)/shard_map/ppermute | solution.py:21
  44.0 24.3 %collective-permute-done.5 = f32[256,1024]{1,0:T(8,128)} collective-permute-done((f32[256,1024]{1,0:T(8,128)}, f32[256,1024]{1,0:T(8,128)}, u32[]{:S(2)}, u32[]{:S(2)}) %collective-permute-start.5) | collective-permute-done | bytes 1048608 | tf_op jit(solution)/shard_map/ppermute | solution.py:30
  70.9 3.6 collective-permute-start.7
  87.5 7.0 %fusion.174 = (f32[256,1024]{1,0:T(8,128)S(1)}, f32[256,1024]{1,0:T(8,128)}) fusion(f32[256,1024]{1,0:T(8,128)} %fusion.75, f32[256,1024]{1,0:T(8,128)} %collective-permute-done.5, f32[258,1026]{1,0:T(8,128)S(1)} %select_maximum_fusion.14, f32[1,1024]{1,0:T(1,128)S(1)} %collective-permute-done.7, f32[1,1024]{1,0:T(1,128)S(1)} %collective-permute-done.6, ...), kind=kLoop, calls=%fused_computation.286 | loop fusion | flops 11272192 | bytes 13738498 | tf_op jit(solution)/shard_map/jit(_where)/select_n | solution.py:99
  95.8 24.9 %collective-permute-done.10 = f32[256,1024]{1,0:T(8,128)S(1)} collective-permute-done((f32[256,1024]{1,0:T(8,128)S(1)}, f32[256,1024]{1,0:T(8,128)S(1)}, u32[]{:S(2)}, u32[]{:S(2)}) %collective-permute-start.10) | collective-permute-done | bytes 1048608 | tf_op jit(solution)/shard_map/ppermute | solution.py:30
  123.6 3.6 collective-permute-start.12
  129.7 3.5 fusion.108
  134.5 25.4 %collective-permute-done.13 = f32[256,1024]{1,0:T(8,128)S(1)} collective-permute-done((f32[256,1024]{1,0:T(8,128)S(1)}, f32[256,1024]{1,0:T(8,128)S(1)}, u32[]{:S(2)}, u32[]{:S(2)}) %collective-permute-start.13) | collective-permute-done | bytes 1048608 | tf_op jit(solution)/shard_map/ppermute | solution.py:30
  162.9 3.6 collective-permute-start.15
  168.9 3.2 fusion.114
  173.5 25.9 %collective-permute-done.16 = f32[256,1024]{1,0:T(8,128)S(1)} collective-permute-done((f32[256,1024]{1,0:T(8,128)S(1)}, f32[256,1024]{1,0:T(8,128)S(1)}, u32[]{:S(2)}, u32[]{:S(2)}) %collective-permute-start.16) | collective-permute-done | bytes 1048608 | tf_op jit(solution)/shard_map/ppermute | solution.py:30
  202.4 3.6 collective-permute-start.18
  208.4 3.5 fusion.120
  213.4 25.7 %collective-permute-done.19 = f32[256,1024]{1,0:T(8,128)S(1)} collective-permute-done((f32[256,1024]{1,0:T(8,128)S(1)}, f32[256,1024]{1,0:T(8,128)S(1)}, u32[]{:S(2)}, u32[]{:S(2)}) %collective-permute-start.19) | collective-permute-done | bytes 1048608 | tf_op jit(solution)/shard_map/ppermute | solution.py:30
  241.1 3.6 collective-permute-start.21
  248.1 25.5 %collective-permute-done.22 = f32[256,1024]{1,0:T(8,128)S(1)} collective-permute-done((f32[256,1024]{1,0:T(8,128)S(1)}, f32[256,1024]{1,0:T(8,128)S(1)}, u32[]{:S(2)}, u32[]{:S(2)}) %collective-permute-start.22) | collective-permute-done | bytes 1048608 | tf_op jit(solution)/shard_map/ppermute | solution.py:30
  275.6 3.6 collective-permute-start.24
  282.7 25.8 %collective-permute-done.25 = f32[256,1024]{1,0:T(8,128)S(1)} collective-permute-done((f32[256,1024]{1,0:T(8,128)S(1)}, f32[256,1024]{1,0:T(8,128)S(1)}, u32[]{:S(2)}, u32[]{:S(2)}) %collective-permute-start.25) | collective-permute-done | bytes 1048608 | tf_op jit(solution)/shard_map/ppermute | solution.py:30
  310.5 3.6 collective-permute-start.27
  317.5 25.8 %collective-permute-done.28 = f32[256,1024]{1,0:T(8,128)S(1)} collective-permute-done((f32[256,1024]{1,0:T(8,128)S(1)}, f32[256,1024]{1,0:T(8,128)S(1)}, u32[]{:S(2)}, u32[]{:S(2)}) %collective-permute-start.28) | collective-permute-done | bytes 1048608 | tf_op jit(solution)/shard_map/ppermute | solution.py:30
  345.3 3.6 collective-permute-start.30
  351.1 4.2 %collective-permute-start.31 = (f32[3,1024]{1,0:T(4,128)S(1)}, f32[3,1024]{1,0:T(4,128)S(1)}, u32[]{:S(2)}, u32[]{:S(2)}) collective-permute-start(f32[3,1024]{1,0:T(4,128)S(1)} %get-tuple-element.6), channel_id=1, source_target_pairs={{0,1},{1,2},{2,3},{4,5},{5,6},{6,7},{8,9},{9,10},{10,11},{12,13},{... | collective-permute-start | bytes 36872 | tf_op jit(solution)/shard_map/ppermute | solution.py:21
  (127 shorter events, 83.3 us)
Async XLA Ops:
  0.6 26.1 %collective-permute-start = (f32[256,1024]{1,0:T(8,128)}, f32[256,1024]{1,0:T(8,128)S(1)}, u32[]{:S(2)}, u32[]{:S(2)}) collective-permute-start(f32[256,1024]{1,0:T(8,128)} %bitcast.56), channel_id=1, source_target_pairs={{0,4},{4,8},{8,12},{12,16},{16,20},{20,24},{24,28},{1,5},{5,9},{9,... | collective-permute-start | bytes 3145736 | tf_op jit(solution)/shard_map/ppermute | solution.py:30
  2.9 30.4 %collective-permute-start.3 = (f32[2,4,1024]{2,1,0:T(4,128)S(1)}, f32[2,4,1024]{2,1,0:T(4,128)S(1)}, u32[]{:S(2)}, u32[]{:S(2)}) collective-permute-start(f32[2,4,1024]{2,1,0:T(4,128)S(1)} %get-tuple-element.4), channel_id=1, source_target_pairs={{0,1},{1,2},{2,3},{4,5},{5,6},{6,7},{8,9},{9,10},{10,11},{12,13},{... | collective-permute-start | bytes 98312 | tf_op jit(solution)/shard_map/ppermute | solution.py:21
  6.6 26.7 %collective-permute-start.4 = (f32[2,4,1024]{2,1,0:T(4,128)S(1)}, f32[2,4,1024]{2,1,0:T(4,128)S(1)}, u32[]{:S(2)}, u32[]{:S(2)}) collective-permute-start(f32[2,4,1024]{2,1,0:T(4,128)S(1)} %get-tuple-element.5), channel_id=1, source_target_pairs={{1,0},{2,1},{3,2},{5,4},{6,5},{7,6},{9,8},{10,9},{11,10},{13,12},{... | collective-permute-start | bytes 98312 | tf_op jit(solution)/shard_map/ppermute | solution.py:22
  26.8 8.3 %collective-permute-start.1 = (f32[4,1024]{1,0:T(4,128)S(1)}, f32[4,1024]{1,0:T(4,128)S(1)}, u32[]{:S(2)}, u32[]{:S(2)}) collective-permute-start(f32[4,1024]{1,0:T(4,128)S(1)} %get-tuple-element.26), channel_id=1, source_target_pairs={{0,1},{1,2},{2,3},{4,5},{5,6},{6,7},{8,9},{9,10},{10,11},{12,13},{... | collective-permute-start | bytes 49160 | tf_op jit(solution)/shard_map/ppermute | solution.py:21
  31.4 5.1 %collective-permute-start.2 = (f32[4,1024]{1,0:T(4,128)S(1)}, f32[4,1024]{1,0:T(4,128)S(1)}, u32[]{:S(2)}, u32[]{:S(2)}) collective-permute-start(f32[4,1024]{1,0:T(4,128)S(1)} %get-tuple-element.27), channel_id=1, source_target_pairs={{1,0},{2,1},{3,2},{5,4},{6,5},{7,6},{9,8},{10,9},{11,10},{13,12},{... | collective-permute-start | bytes 49160 | tf_op jit(solution)/shard_map/ppermute | solution.py:22
  42.7 25.6 %collective-permute-start.5 = (f32[256,1024]{1,0:T(8,128)}, f32[256,1024]{1,0:T(8,128)}, u32[]{:S(2)}, u32[]{:S(2)}) collective-permute-start(f32[256,1024]{1,0:T(8,128)} %fusion.75), channel_id=1, source_target_pairs={{0,4},{4,8},{8,12},{12,16},{16,20},{20,24},{24,28},{1,5},{5,9},{9,... | collective-permute-start | bytes 3145736 | tf_op jit(solution)/shard_map/ppermute | solution.py:30
  69.0 10.9 %collective-permute-start.6 = (f32[1,1024]{1,0:T(1,128)S(1)}, f32[1,1024]{1,0:T(1,128)S(1)}, u32[]{:S(2)}, u32[]{:S(2)}) collective-permute-start(f32[1,1024]{1,0:T(1,128)S(1)} %get-tuple-element.25), channel_id=1, source_target_pairs={{1,0},{2,1},{3,2},{5,4},{6,5},{7,6},{9,8},{10,9},{11,10},{13,12},{... | collective-permute-start | bytes 12296 | tf_op jit(solution)/shard_map/ppermute | solution.py:22
  70.9 9.0 %collective-permute-start.7 = (f32[1,1024]{1,0:T(1,128)S(1)}, f32[1,1024]{1,0:T(1,128)S(1)}, u32[]{:S(2)}, u32[]{:S(2)}) collective-permute-start(f32[1,1024]{1,0:T(1,128)S(1)} %get-tuple-element.24), channel_id=1, source_target_pairs={{0,1},{1,2},{2,3},{4,5},{5,6},{6,7},{8,9},{9,10},{10,11},{12,13},{... | collective-permute-start | bytes 12296 | tf_op jit(solution)/shard_map/ppermute | solution.py:21
  75.4 6.2 %collective-permute-start.8 = (f32[4,1024]{1,0:T(4,128)S(1)}, f32[4,1024]{1,0:T(4,128)S(1)}, u32[]{:S(2)}, u32[]{:S(2)}) collective-permute-start(f32[4,1024]{1,0:T(4,128)S(1)} %get-tuple-element.22), channel_id=1, source_target_pairs={{0,1},{1,2},{2,3},{4,5},{5,6},{6,7},{8,9},{9,10},{10,11},{12,13},{... | collective-permute-start | bytes 49160 | tf_op jit(solution)/shard_map/ppermute | solution.py:21
  94.5 26.1 %collective-permute-start.10 = (f32[256,1024]{1,0:T(8,128)S(1)}, f32[256,1024]{1,0:T(8,128)S(1)}, u32[]{:S(2)}, u32[]{:S(2)}) collective-permute-start(f32[256,1024]{1,0:T(8,128)S(1)} %get-tuple-element.2), channel_id=1, source_target_pairs={{0,4},{4,8},{8,12},{12,16},{16,20},{20,24},{24,28},{1,5},{5,9},{9,... | collective-permute-start | bytes 3145736 | tf_op jit(solution)/shard_map/ppermute | solution.py:30
  121.7 5.6 %collective-permute-start.11 = (f32[1,1024]{1,0:T(1,128)S(1)}, f32[1,1024]{1,0:T(1,128)S(1)}, u32[]{:S(2)}, u32[]{:S(2)}) collective-permute-start(f32[1,1024]{1,0:T(1,128)S(1)} %get-tuple-element.21), channel_id=1, source_target_pairs={{1,0},{2,1},{3,2},{5,4},{6,5},{7,6},{9,8},{10,9},{11,10},{13,12},{... | collective-permute-start | bytes 12296 | tf_op jit(solution)/shard_map/ppermute | solution.py:22
  133.2 26.7 %collective-permute-start.13 = (f32[256,1024]{1,0:T(8,128)S(1)}, f32[256,1024]{1,0:T(8,128)S(1)}, u32[]{:S(2)}, u32[]{:S(2)}) collective-permute-start(f32[256,1024]{1,0:T(8,128)S(1)} %fusion.108), channel_id=1, source_target_pairs={{0,4},{4,8},{8,12},{12,16},{16,20},{20,24},{24,28},{1,5},{5,9},{9,... | collective-permute-start | bytes 3145736 | tf_op jit(solution)/shard_map/ppermute | solution.py:30
  160.9 5.6 %collective-permute-start.14 = (f32[1,1024]{1,0:T(1,128)S(1)}, f32[1,1024]{1,0:T(1,128)S(1)}, u32[]{:S(2)}, u32[]{:S(2)}) collective-permute-start(f32[1,1024]{1,0:T(1,128)S(1)} %get-tuple-element.19), channel_id=1, source_target_pairs={{1,0},{2,1},{3,2},{5,4},{6,5},{7,6},{9,8},{10,9},{11,10},{13,12},{... | collective-permute-start | bytes 12296 | tf_op jit(solution)/shard_map/ppermute | solution.py:22
  172.2 27.2 %collective-permute-start.16 = (f32[256,1024]{1,0:T(8,128)S(1)}, f32[256,1024]{1,0:T(8,128)S(1)}, u32[]{:S(2)}, u32[]{:S(2)}) collective-permute-start(f32[256,1024]{1,0:T(8,128)S(1)} %fusion.114), channel_id=1, source_target_pairs={{0,4},{4,8},{8,12},{12,16},{16,20},{20,24},{24,28},{1,5},{5,9},{9,... | collective-permute-start | bytes 3145736 | tf_op jit(solution)/shard_map/ppermute | solution.py:30
  200.4 5.6 %collective-permute-start.17 = (f32[1,1024]{1,0:T(1,128)S(1)}, f32[1,1024]{1,0:T(1,128)S(1)}, u32[]{:S(2)}, u32[]{:S(2)}) collective-permute-start(f32[1,1024]{1,0:T(1,128)S(1)} %get-tuple-element.17), channel_id=1, source_target_pairs={{1,0},{2,1},{3,2},{5,4},{6,5},{7,6},{9,8},{10,9},{11,10},{13,12},{... | collective-permute-start | bytes 12296 | tf_op jit(solution)/shard_map/ppermute | solution.py:22
  211.9 27.3 %collective-permute-start.19 = (f32[256,1024]{1,0:T(8,128)S(1)}, f32[256,1024]{1,0:T(8,128)S(1)}, u32[]{:S(2)}, u32[]{:S(2)}) collective-permute-start(f32[256,1024]{1,0:T(8,128)S(1)} %fusion.120), channel_id=1, source_target_pairs={{0,4},{4,8},{8,12},{12,16},{16,20},{20,24},{24,28},{1,5},{5,9},{9,... | collective-permute-start | bytes 3145736 | tf_op jit(solution)/shard_map/ppermute | solution.py:30
  239.1 5.6 %collective-permute-start.20 = (f32[1,1024]{1,0:T(1,128)S(1)}, f32[1,1024]{1,0:T(1,128)S(1)}, u32[]{:S(2)}, u32[]{:S(2)}) collective-permute-start(f32[1,1024]{1,0:T(1,128)S(1)} %get-tuple-element.15), channel_id=1, source_target_pairs={{1,0},{2,1},{3,2},{5,4},{6,5},{7,6},{9,8},{10,9},{11,10},{13,12},{... | collective-permute-start | bytes 12296 | tf_op jit(solution)/shard_map/ppermute | solution.py:22
  246.8 26.8 %collective-permute-start.22 = (f32[256,1024]{1,0:T(8,128)S(1)}, f32[256,1024]{1,0:T(8,128)S(1)}, u32[]{:S(2)}, u32[]{:S(2)}) collective-permute-start(f32[256,1024]{1,0:T(8,128)S(1)} %fusion.126), channel_id=1, source_target_pairs={{0,4},{4,8},{8,12},{12,16},{16,20},{20,24},{24,28},{1,5},{5,9},{9,... | collective-permute-start | bytes 3145736 | tf_op jit(solution)/shard_map/ppermute | solution.py:30
  273.7 5.6 %collective-permute-start.23 = (f32[1,1024]{1,0:T(1,128)S(1)}, f32[1,1024]{1,0:T(1,128)S(1)}, u32[]{:S(2)}, u32[]{:S(2)}) collective-permute-start(f32[1,1024]{1,0:T(1,128)S(1)} %get-tuple-element.13), channel_id=1, source_target_pairs={{1,0},{2,1},{3,2},{5,4},{6,5},{7,6},{9,8},{10,9},{11,10},{13,12},{... | collective-permute-start | bytes 12296 | tf_op jit(solution)/shard_map/ppermute | solution.py:22
  281.4 27.1 %collective-permute-start.25 = (f32[256,1024]{1,0:T(8,128)S(1)}, f32[256,1024]{1,0:T(8,128)S(1)}, u32[]{:S(2)}, u32[]{:S(2)}) collective-permute-start(f32[256,1024]{1,0:T(8,128)S(1)} %fusion.132), channel_id=1, source_target_pairs={{0,4},{4,8},{8,12},{12,16},{16,20},{20,24},{24,28},{1,5},{5,9},{9,... | collective-permute-start | bytes 3145736 | tf_op jit(solution)/shard_map/ppermute | solution.py:30
  308.5 5.6 %collective-permute-start.26 = (f32[1,1024]{1,0:T(1,128)S(1)}, f32[1,1024]{1,0:T(1,128)S(1)}, u32[]{:S(2)}, u32[]{:S(2)}) collective-permute-start(f32[1,1024]{1,0:T(1,128)S(1)} %get-tuple-element.11), channel_id=1, source_target_pairs={{1,0},{2,1},{3,2},{5,4},{6,5},{7,6},{9,8},{10,9},{11,10},{13,12},{... | collective-permute-start | bytes 12296 | tf_op jit(solution)/shard_map/ppermute | solution.py:22
  316.2 27.1 %collective-permute-start.28 = (f32[256,1024]{1,0:T(8,128)S(1)}, f32[256,1024]{1,0:T(8,128)S(1)}, u32[]{:S(2)}, u32[]{:S(2)}) collective-permute-start(f32[256,1024]{1,0:T(8,128)S(1)} %fusion.138), channel_id=1, source_target_pairs={{0,4},{4,8},{8,12},{12,16},{16,20},{20,24},{24,28},{1,5},{5,9},{9,... | collective-permute-start | bytes 3145736 | tf_op jit(solution)/shard_map/ppermute | solution.py:30
  343.4 5.6 %collective-permute-start.29 = (f32[1,1024]{1,0:T(1,128)S(1)}, f32[1,1024]{1,0:T(1,128)S(1)}, u32[]{:S(2)}, u32[]{:S(2)}) collective-permute-start(f32[1,1024]{1,0:T(1,128)S(1)} %get-tuple-element.9), channel_id=1, source_target_pairs={{1,0},{2,1},{3,2},{5,4},{6,5},{7,6},{9,8},{10,9},{11,10},{13,12},{... | collective-permute-start | bytes 12296 | tf_op jit(solution)/shard_map/ppermute | solution.py:22
  351.1 6.1 %collective-permute-start.31 = (f32[3,1024]{1,0:T(4,128)S(1)}, f32[3,1024]{1,0:T(4,128)S(1)}, u32[]{:S(2)}, u32[]{:S(2)}) collective-permute-start(f32[3,1024]{1,0:T(4,128)S(1)} %get-tuple-element.6), channel_id=1, source_target_pairs={{0,1},{1,2},{2,3},{4,5},{5,6},{6,7},{8,9},{9,10},{10,11},{12,13},{... | collective-permute-start | bytes 36872 | tf_op jit(solution)/shard_map/ppermute | solution.py:21
  (28 other events, 195.8 us)
where the time goes:
time: 369 us; the launch traced here: 365 us
  waiting for transfers between devices  232 us (63%)
  starting transfers between devices  79 us (21%)
  other arithmetic  47.6 us (13%)
  local copies, waits for them, and re-layouts  5.19 us (1%)
    ppermute x9, waiting for transfers between devices, from_behind(): lax.ppermute(value, axis, [(source, source + steps) for source in range(i...  222 us
    ppermute x12, starting transfers between devices, extended(): before = lax.ppermute(last, axis, up)  43.5 us
    ppermute x12, starting transfers between devices, extended(): after = lax.ppermute(initial, axis, down)  23.7 us
    select_n x8, other arithmetic, local(): coarse = jnp.where(active, updated, coarse)  21 us
    ppermute x9, starting transfers between devices, from_behind(): lax.ppermute(value, axis, [(source, source + steps) for source in range(i...  11.8 us
    concatenate x12, other arithmetic, extended(): shard = jnp.concatenate([before, shard, after], axis=dim)  11.5 us
    select_n x8, other arithmetic, deep_step(): return jnp.where(inside, stepped, jnp.zeros_like(stepped))  9.82 us
  transfers between devices with their start and end apart: 33, of which 19 were waited for; matrix products, arithmetic and copies ran while one was open for 1% of the time, Pallas kernels for 0%

commit v1 on v0

--- a/solution.py
+++ b/solution.py
@@ -1,6 +1,9 @@
+import functools
 import jax
 import jax.numpy as jnp
 from jax import lax
+from jax.experimental import pallas as pl
+from jax.experimental.pallas import tpu as pltpu
 from jax.sharding import PartitionSpec as P
 
 STEPS = 4
@@ -9,6 +12,370 @@
 
 
 DIFFUSION = 0.05
+PAD = 8
+CHUNK = 16
+MESH = pl.DeviceIdType.MESH
+
+
+def step_rows(src, kw, rw, low, count, shift, scale, cols):
+    band = src[pl.ds(pl.multiple_of(low - PAD, 8), count + 2 * PAD), :]
+    centre = band[PAD : PAD + count]
+    above = band[PAD - 1 : PAD - 1 + count]
+    below = band[PAD + 1 : PAD + 1 + count]
+    width = centre.shape[1]
+    left = jnp.where(cols == 0, 0.0, pltpu.roll(centre, 1, 1))
+    right = jnp.where(cols == width - 1, 0.0, pltpu.roll(centre, width - 1, 1))
+    where = pl.ds(pl.multiple_of(low + shift, 8), count)
+    laplace = (above + below) + (left + right) - 4.0 * centre
+    change = kw[where, :] * laplace + rw[where, :] * (centre - centre * centre * centre)
+    return centre + (change if scale == 1.0 else scale * change)
+
+
+def kernel(
+    points, strips, guess, kappa, rate, c_out, f_out,
+    kw, rw, ga, gb, x_ref, ya, yb, z_ref, da, db, cr, vo, ve, vw, u1, u2, kh,
+    k_send, k_recv, g_send, g_recv, c_send, c_recv, f_send, f_recv,
+):
+    rows, width = kappa.shape
+    half = rows // 2
+    wide = ga.shape[0]
+    halo = (wide - 2 * PAD - half) // 2
+    chunks = (wide - 2 * PAD) // CHUNK
+    skipped = halo // CHUNK
+    full = vw.shape[0]
+    pairs = points // 2
+    tm, s = lax.axis_index("tm"), lax.axis_index("space")
+    p, b = tm // 2, tm % 2
+    coarse_scale = float(STEPS)
+    cols = lax.broadcasted_iota(jnp.int32, (CHUNK, width), 1)
+    shift = b * half
+    partner = p * 2 + (1 - b)
+
+    later, earlier = p < pairs - 1, p > 0
+    below, above = s < strips - 1, s > 0
+    even, odd = b == 0, b == 1
+
+    targets = [
+        (below, (tm, s + 1)), (above, (tm, s - 1)), (s >= 0, (partner, s)),
+        (even & above, (tm + 1, s - 1)), (later, (tm + 2, s)),
+        (odd & later, (tm + 1, s)), (odd & later & below, (tm + 1, s + 1)),
+        (odd & later & above, (tm + 2, s - 1)),
+    ]
+    sources = [
+        (below, (tm, s + 1)), (above, (tm, s - 1)), (s >= 0, (partner, s)),
+        (odd & below, (tm - 1, s + 1)), (earlier, (tm - 2, s)),
+        (even & earlier, (tm - 1, s)), (even & earlier & above, (tm - 1, s - 1)),
+        (odd & earlier & below, (tm - 2, s + 1)),
+    ]
+    barrier = pltpu.get_barrier_semaphore()
+    for condition, device in sources:
+        @pl.when(condition)
+        def _(device=device):
+            pl.semaphore_signal(barrier, inc=1, device_id=device, device_id_type=MESH)
+    count = sum(condition.astype(jnp.int32) for condition, _ in targets)
+    pl.semaphore_wait(barrier, count)
+
+    def copy(src, dst, send, recv, device):
+        return pltpu.make_async_remote_copy(
+            src_ref=src, dst_ref=dst, send_sem=send, recv_sem=recv,
+            device_id=device, device_id_type=MESH,
+        )
+
+    main = half + halo
+    first, last = pl.ds(0, halo), pl.ds(rows - halo, halo)
+    upper, lower = pl.ds(PAD, halo), pl.ds(PAD + main, halo)
+    main_even, main_odd = pl.ds(PAD + halo, main), pl.ds(PAD, main)
+    head, tail = pl.ds(0, main), pl.ds(rows - main, main)
+    halves = [
+        (below, copy(kappa.at[last], kh.at[0], k_send.at[0], k_recv.at[0], (tm, s + 1))),
+        (below, copy(rate.at[last], kh.at[1], k_send.at[1], k_recv.at[1], (tm, s + 1))),
+        (above, copy(kappa.at[first], kh.at[2], k_send.at[2], k_recv.at[2], (tm, s - 1))),
+        (above, copy(rate.at[first], kh.at[3], k_send.at[3], k_recv.at[3], (tm, s - 1))),
+    ]
+    own = guess.at[0]
+    fields = [
+        (even & below, copy(own.at[last], gb.at[upper], g_send.at[0], g_recv.at[0], (tm, s + 1))),
+        (even & above, copy(own.at[first], gb.at[lower], g_send.at[1], g_recv.at[0], (tm + 1, s - 1))),
+        (odd & later & below, copy(own.at[last], ga.at[upper], g_send.at[0], g_recv.at[2], (tm + 1, s + 1))),
+        (odd & later & above, copy(own.at[first], ga.at[lower], g_send.at[1], g_recv.at[2], (tm + 2, s - 1))),
+        (even, copy(own.at[tail], gb.at[main_odd], g_send.at[2], g_recv.at[1], (partner, s))),
+        (odd & later, copy(own.at[tail], ga.at[main_odd], g_send.at[2], g_recv.at[3], (tm + 2, s))),
+        (odd & later, copy(own.at[head], ga.at[main_even], g_send.at[3], g_recv.at[3], (tm + 1, s))),
+    ]
+    for condition, transfer in halves + fields:
+        @pl.when(condition)
+        def _(transfer=transfer):
+            transfer.start()
+
+    zeros = jnp.zeros((PAD, width), jnp.float32)
+    for ref in (ga, gb, x_ref, ya, yb, z_ref, cr, vo, vw, u1, u2, kw, rw):
+        ref[pl.ds(0, PAD), :] = zeros
+        ref[pl.ds(ref.shape[0] - PAD, PAD), :] = zeros
+    blank = jnp.zeros((halo, width), jnp.float32)
+
+    def fill(index, carry):
+        start = pl.multiple_of(index * CHUNK, CHUNK)
+        at = pl.multiple_of(start + PAD + halo, 8)
+        kw[pl.ds(at, CHUNK), :] = DIFFUSION * kappa[pl.ds(start, CHUNK), :]
+        rw[pl.ds(at, CHUNK), :] = rate[pl.ds(start, CHUNK), :]
+        return carry
+
+    lax.fori_loop(0, rows // CHUNK, fill, 0)
+
+    @pl.when(even)
+    def _():
+        def place(index, carry):
+            start = pl.multiple_of(index * CHUNK, CHUNK)
+            at = pl.multiple_of(start + PAD + halo, 8)
+            gb[pl.ds(at, CHUNK), :] = guess[0, pl.ds(start, CHUNK), :]
+            return carry
+
+        lax.fori_loop(0, main // CHUNK, place, 0)
+
+    @pl.when(even & ~above)
+    def _():
+        ga[upper, :] = blank
+        gb[upper, :] = blank
+
+    @pl.when(odd & ~below)
+    def _():
+        ga[lower, :] = blank
+        gb[lower, :] = blank
+
+    end = pl.ds(full - PAD - halo, halo)
+
+    @pl.when(above)
+    def _():
+        halves[0][1].wait_recv()
+        halves[1][1].wait_recv()
+        kw[upper, :] = DIFFUSION * kh[0]
+        rw[upper, :] = kh[1]
+
+    @pl.when(~above)
+    def _():
+        kw[upper, :] = blank
+        rw[upper, :] = blank
+
+    @pl.when(below)
+    def _():
+        halves[2][1].wait_recv()
+        halves[3][1].wait_recv()
+        kw[end, :] = DIFFUSION * kh[2]
+        rw[end, :] = kh[3]
+
+    @pl.when(~below)
+    def _():
+        kw[end, :] = blank
+        rw[end, :] = blank
+
+    def chunk(index):
+        return pl.ds(pl.multiple_of(index * CHUNK + PAD, 8), CHUNK)
+
+    def advance(src, index, scale):
+        return step_rows(src, kw, rw, index * CHUNK + PAD, CHUNK, shift, scale, cols)
+
+    def sweep(src, dst):
+        def body(index, carry):
+            dst[chunk(index), :] = advance(src, index, 1.0)
+            return carry
+
+        lax.fori_loop(0, chunks, body, 0)
+
+    def march(src, scratch, dst, times):
+        for turn in range(times):
+            out = dst if (times - 1 - turn) % 2 == 0 else scratch
+            sweep(src, out)
+            src = out
+
+    def defects(field, relaxed, out, whole):
+        march(field, x_ref, relaxed, STEPS)
+        march(relaxed, z_ref, x_ref, STEPS - 1)
+
+        def body(index, carry):
+            fine = advance(x_ref, index, 1.0)
+            coarse = advance(relaxed, index, coarse_scale)
+            out[chunk(index), :] = jnp.where(whole, fine, fine - coarse)
+            return carry
+
+        lax.fori_loop(0, chunks, body, 0)
+
+    @pl.when(even & above)
+    def _():
+        fields[0][1].wait_recv()
+
+    @pl.when(odd & below)
+    def _():
+        fields[1][1].wait_recv()
+
+    @pl.when(odd)
+    def _():
+        fields[4][1].wait_recv()
+
+    defects(gb, yb, db, p == 0)
+
+    @pl.when(earlier)
+    def _():
+        @pl.when(even & above)
+        def _():
+            fields[2][1].wait_recv()
+
+        @pl.when(odd & below)
+        def _():
+            fields[3][1].wait_recv()
+
+        @pl.when(even)
+        def _():
+            fields[6][1].wait_recv()
+
+        @pl.when(odd)
+        def _():
+            fields[5][1].wait_recv()
+
+        defects(ga, ya, da, p < 0)
+
+    def chain(index):
+        part = chunk(index)
+        return copy(ve.at[part], cr.at[part], c_send.at[index], c_recv.at[index], (tm + 2, s))
+
+    def target(index, side):
+        return pl.ds(pl.multiple_of(index * CHUNK + PAD + side * half, 8), CHUNK)
+
+    kept = chunks - skipped
+
+    def forward(index, src):
+        return copy(
+            src.at[chunk(index)], vw.at[target(index, b)], f_send.at[index], f_recv.at[index],
+            (partner, s),
+        )
+
+    def hand_over(index):
+        @pl.when(even & (index < kept))
+        def _():
+            forward(index, vo).start()
+            vw[target(index, 0), :] = cr[chunk(index), :]
+
+        @pl.when(odd & (index >= skipped))
+        def _():
+            forward(index, cr).start()
+            vw[target(index, 1), :] = vo[chunk(index), :]
+
+    @pl.when(p == 0)
+    def _():
+        def body(index, carry):
+            part = chunk(index)
+            ve[part, :] = db[part, :]
+            chain(index).start()
+            vo[part, :] = yb[part, :]
+            cr[part, :] = gb[part, :]
+            hand_over(index)
+            return carry
+
+        lax.fori_loop(0, chunks, body, 0)
+
+    @pl.when(earlier)
+    def _():
+        def body(index, carry):
+            @pl.when(index < chunks)
+            def _():
+                chain(index).wait_recv()
+
+            @pl.when((index >= 1) & (index <= chunks))
+            def _():
+                now = index - 1
+                vo[chunk(now), :] = advance(cr, now, coarse_scale) + da[chunk(now), :]
+
+            @pl.when((index >= 2) & later)
+            def _():
+                now = index - 2
+                ve[chunk(now), :] = advance(vo, now, coarse_scale) + db[chunk(now), :]
+                chain(now).start()
+
+            @pl.when((index >= 1) & (index <= chunks))
+            def _():
+                hand_over(index - 1)
+
+            return carry
+
+        lax.fori_loop(0, chunks + 2, body, 0)
+
+    def collect(index, carry):
+        forward(index + skipped * (1 - b), vo).wait_recv()
+        return carry
+
+    lax.fori_loop(0, kept, collect, 0)
+
+    def wide_step(src, dst, low, offset, blocks):
+        def body(index, carry):
+            start = index * CHUNK + low
+            out = pl.ds(pl.multiple_of(start - offset, 8), CHUNK)
+            dst[out, :] = step_rows(src, kw, rw, start, CHUNK, 0, 1.0, cols)
+            return carry
+
+        lax.fori_loop(0, blocks, body, 0)
+
+    src = vw
+    for turn in range(STEPS - 2):
+        out = u1 if turn % 2 == 0 else u2
+        wide_step(src, out, PAD, 0, (full - 2 * PAD) // CHUNK)
+        src = out
+
+    def finish(index, carry):
+        start = index * CHUNK
+        low = start + PAD + halo
+        out = pl.ds(pl.multiple_of(start, CHUNK), CHUNK)
+        f_out[0, out, :] = step_rows(src, kw, rw, low, CHUNK, 0, 1.0, cols)
+        c_out[0, out, :] = vw[pl.ds(pl.multiple_of(low, 8), CHUNK), :]
+        return carry
+
+    lax.fori_loop(0, rows // CHUNK, finish, 0)
+
+    for condition, transfer in halves + fields:
+        @pl.when(condition)
+        def _(transfer=transfer):
+            transfer.wait_send()
+
+    @pl.when(later)
+    def _():
+        def body(index, carry):
+            chain(index).wait_send()
+            return carry
+
+        lax.fori_loop(0, chunks, body, 0)
+
+    def sent(index, carry):
+        forward(index + skipped * b, vo).wait_send()
+        return carry
+
+    lax.fori_loop(0, kept, sent, 0)
+
+
+def chained(points, strips, guess, kappa, rate):
+    rows, width = kappa.shape
+    halo = halo_of(points)
+    wide = rows // 2 + 2 * halo + 2 * PAD
+    full = rows + 2 * halo + 2 * PAD
+    chunks = (wide - 2 * PAD) // CHUNK
+    f32 = jnp.float32
+    part, whole = pltpu.VMEM((wide, width), f32), pltpu.VMEM((full, width), f32)
+    dma = pltpu.SemaphoreType.DMA
+    vmem = pl.BlockSpec(memory_space=pltpu.VMEM)
+    return pl.pallas_call(
+        functools.partial(kernel, points, strips),
+        out_shape=[jax.ShapeDtypeStruct(guess.shape, f32)] * 2,
+        in_specs=[vmem] * 3,
+        out_specs=[vmem] * 2,
+        scratch_shapes=[whole, whole] + [part] * 11 + [whole] * 3
+        + [pltpu.VMEM((4, halo, width), f32)]
+        + [dma((4,))] * 4 + [dma((chunks,))] * 4,
+        compiler_params=pltpu.CompilerParams(
+            collective_id=0, has_side_effects=True, vmem_limit_bytes=48 * 2**20
+        ),
+    )(guess, kappa, rate)
+
+
+def halo_of(points):
+    needed = 2 * STEPS + max(points - 3, 0) + STEPS - 1
+    return -(-needed // CHUNK) * CHUNK
 
 
 def extended(shard, sides, width):
@@ -102,8 +469,17 @@
 
 
 def solution(mesh):
+    points, strips = mesh.shape["tm"], mesh.shape["space"]
+
+    def run(guess, kappa, rate):
+        half = kappa.shape[0] // 2
+        settled = points <= GROUP * SWEEPS and points % 2 == 0 and points >= 4
+        if settled and half % CHUNK == 0 and halo_of(points) <= half:
+            return tuple(chained(points, strips, guess, kappa, rate))
+        return local(guess, kappa, rate)
+
     return jax.shard_map(
-        local,
+        run,
         mesh=mesh,
         in_specs=(P("tm", "space", None), P("space", None), P("space", None)),
         out_specs=(P("tm", "space", None), P("tm", "space", None)),

time: 369 us -> 80 us (0.22)
  waiting for transfers between devices: 232 us -> 0 us
  starting transfers between devices: 79 us -> 0 us
  Pallas kernels: 0 us -> 73.5 us
  other arithmetic: 47.6 us -> 0 us
    ppermute x33 -> x0, waiting for transfers between devices: 232 us -> none  [the longest x9 222 us: from_behind(): lax.ppermute(value, axis, [(source, source + steps) for source in range(i...]
    ppermute x33 -> x0, starting transfers between devices: 79 us -> none  [the longest x12 43.5 us: extended(): before = lax.ppermute(last, axis, up)]
    pallas_call x0 -> x1, Pallas kernels: none -> 73.5 us  [chained(): pl.pallas_call(functools.partial(kernel, points, strips), out_shape=[jax....]
    select_n x17 -> x0, other arithmetic: 33 us -> none  [the longest x8 21 us: local(): coarse = jnp.where(active, updated, coarse)]
    concatenate x12 -> x0, other arithmetic: 11.5 us -> none  [extended(): shard = jnp.concatenate([before, shard, after], axis=dim)]
  transfers between devices with their start and end apart: 33 -> 0, of which waited for: 19 -> 0; matrix products, arithmetic and copies ran while one was open for 1% -> 0% of each run, Pallas kernels for 0% -> 0%
where the time goes in v1:
time: 80 us; the launch traced here: 79.7 us
  Pallas kernels  73.5 us (92%)
  local copies, waits for them, and re-layouts  5.61 us (7%)
    pallas_call x1, Pallas kernels, chained(): pl.pallas_call(functools.partial(kernel, points, strips), out_shape=[jax....  73.5 us
    unnamed x8, local copies, waits for them, and re-layouts  5.61 us

profile of v1, /device:TPU:27, one launch (start us, length us, event | category | flops | bytes accessed | tf_op | source)
XLA Modules:
  0.0 79.7 jit_solution(14461048669280925427)
XLA Ops:
  0.6 0.0 copy-start
  0.6 1.2 %copy-done = f32[1,256,1024]{2,1,0:T(8,128)S(1)} copy-done((f32[1,256,1024]{2,1,0:T(8,128)S(1)}, f32[1,256,1024]{2,1,0:T(8,128)}, u32[]{:S(2)}) %copy-start) | copy-done | bytes 1048600
  1.9 0.0 copy-start.1
  1.9 1.2 %copy-done.1 = f32[256,1024]{1,0:T(8,128)S(1)} copy-done((f32[256,1024]{1,0:T(8,128)S(1)}, f32[256,1024]{1,0:T(8,128)}, u32[]{:S(2)}) %copy-start.1) | copy-done | bytes 1048600
  3.1 0.0 copy-start.2
  3.1 1.2 %copy-done.2 = f32[256,1024]{1,0:T(8,128)S(1)} copy-done((f32[256,1024]{1,0:T(8,128)S(1)}, f32[256,1024]{1,0:T(8,128)}, u32[]{:S(2)}) %copy-start.2) | copy-done | bytes 1048600
  4.3 73.5 %shard_map.50 = (f32[1,256,1024]{2,1,0:T(8,128)S(1)}, f32[1,256,1024]{2,1,0:T(8,128)S(1)}) custom-call(f32[1,256,1024]{2,1,0:T(8,128)S(1)} %copy-done, f32[256,1024]{1,0:T(8,128)S(1)} %copy-done.1, f32[256,1024]{1,0:T(8,128)S(1)} %copy-done.2), custom_call_target="tpu_custom_call" | custom-call | tf_op jit(solution)/shard_map/pallas_call | solution.py:362
  77.8 1.0 %copy.7 = f32[1,256,1024]{2,1,0:T(8,128)} copy(f32[1,256,1024]{2,1,0:T(8,128)S(1)} %get-tuple-element.4) | data formatting | bytes 2097152
  78.8 1.0 %copy.8 = f32[1,256,1024]{2,1,0:T(8,128)} copy(f32[1,256,1024]{2,1,0:T(8,128)S(1)} %get-tuple-element.5) | data formatting | bytes 2097152
Async XLA Ops:
  0.6 1.2 %copy-start = (f32[1,256,1024]{2,1,0:T(8,128)S(1)}, f32[1,256,1024]{2,1,0:T(8,128)}, u32[]{:S(2)}) copy-start(f32[1,256,1024]{2,1,0:T(8,128)} %guess.1) | copy-start | bytes 3145732
  1.9 1.2 %copy-start.1 = (f32[256,1024]{1,0:T(8,128)S(1)}, f32[256,1024]{1,0:T(8,128)}, u32[]{:S(2)}) copy-start(f32[256,1024]{1,0:T(8,128)} %kappa.1) | copy-start | bytes 3145732
  3.1 1.2 %copy-start.2 = (f32[256,1024]{1,0:T(8,128)S(1)}, f32[256,1024]{1,0:T(8,128)}, u32[]{:S(2)}) copy-start(f32[256,1024]{1,0:T(8,128)} %rate.1) | copy-start | bytes 3145732

commit v2 on v1

v2 whole, which is shorter than its diff:
```python
import functools
import jax
import jax.numpy as jnp
from jax import lax
from jax.experimental import pallas as pl
from jax.experimental.pallas import tpu as pltpu
from jax.sharding import PartitionSpec as P

STEPS = 4
GROUP = 4
SWEEPS = 2


DIFFUSION = 0.05
PAD = 8
CHUNK = 8
LANES = 128
MESH = pl.DeviceIdType.MESH


def block_of(rows):
    return max(size for size in range(8, min(rows, 136) + 1, 8) if rows % size == 0)


def kernel(
    points, strips, guess, kappa, rate, c_out, f_out,
    kw, rw, aw, ga, gb, x_ref, ya, yb, z_ref, w_ref, da, db, cr, vo, ve, vw, u1, u2,
    local_sem, k_send, k_recv, g_send, g_recv, c_send, c_recv, f_send, f_recv,
):
    rows, width = kappa.shape
    tiles = width // LANES
    half = rows // 2
    wide = ga.shape[1]
    full = vw.shape[1]
    halo = (wide - 2 * PAD - half) // 2
    margin = halo - 2 * STEPS
    chunks = (half + 2 * margin) // CHUNK
    skipped = margin // CHUNK
    kept = chunks - skipped
    pairs = points // 2
    tm, s = lax.axis_index("tm"), lax.axis_index("space")
    p, b = tm // 2, tm % 2
    coarse_scale = float(STEPS)
    shift = b * half
    partner = p * 2 + (1 - b)

    later, earlier = p < pairs - 1, p > 0
    below, above = s < strips - 1, s > 0
    even, odd = b == 0, b == 1

    targets = [
        (below, (tm, s + 1)), (above, (tm, s - 1)), (s >= 0, (partner, s)),
        (even & above, (tm + 1, s - 1)), (later, (tm + 2, s)),
        (odd & later, (tm + 1, s)), (odd & later & below, (tm + 1, s + 1)),
        (odd & later & above, (tm + 2, s - 1)),
    ]
    sources = [
        (below, (tm, s + 1)), (above, (tm, s - 1)), (s >= 0, (partner, s)),
        (odd & below, (tm - 1, s + 1)), (earlier, (tm - 2, s)),
        (even & earlier, (tm - 1, s)), (even & earlier & above, (tm - 1, s - 1)),
        (odd & earlier & below, (tm - 2, s + 1)),
    ]
    barrier = pltpu.get_barrier_semaphore()
    for condition, device in sources:
        @pl.when(condition)
        def _(device=device):
            pl.semaphore_signal(barrier, inc=1, device_id=device, device_id_type=MESH)

    main = half + halo
    first, last = (0, halo), (rows - halo, halo)
    head, tail = (0, main), (rows - main, main)
    upper, lower = pl.ds(PAD, halo), pl.ds(PAD + main, halo)
    main_even, main_odd = pl.ds(PAD + halo, main), pl.ds(PAD, main)
    end = pl.ds(PAD + halo + rows, halo)
    middle = pl.ds(PAD + halo, rows)
    own = guess.at[0]

    def columns(src, part):
        start, count = part
        return [src.at[pl.ds(start, count), pl.ds(t * LANES, LANES)] for t in range(tiles)]

    def fetch(src, part, dst, place, sem):
        def start():
            for t, column in enumerate(columns(src, part)):
                pltpu.make_async_copy(column, dst.at[t, place], sem).start()

        def wait():
            pltpu.make_async_copy(dst.at[:, place], dst.at[:, place], sem).wait()

        return start, wait

    def copy(src, dst, send, recv, device):
        return pltpu.make_async_remote_copy(
            src_ref=src, dst_ref=dst, send_sem=send, recv_sem=recv,
            device_id=device, device_id_type=MESH,
        )

    class Send:
        def __init__(self, src, part, dst, place, send, recv, device):
            self.start_all = [
                copy(column, dst.at[t, place], send, recv, device)
                for t, column in enumerate(columns(src, part))
            ]
            self.whole = copy(dst.at[:, place], dst.at[:, place], send, recv, device)

        def start(self):
            for one in self.start_all:
                one.start()

        def wait_recv(self):
            self.whole.wait_recv()

        def wait_send(self):
            self.whole.wait_send()

    k_local = fetch(kappa, (0, rows), kw, middle, local_sem.at[0])
    r_local = fetch(rate, (0, rows), rw, middle, local_sem.at[1])
    g_local = fetch(own, head, gb, main_even, local_sem.at[2])
    k_local[0]()
    r_local[0]()

    @pl.when(even)
    def _():
        g_local[0]()

    sends = [
        (below, Send(kappa, last, kw, upper, k_send.at[0], k_recv.at[0], (tm, s + 1))),
        (below, Send(rate, last, rw, upper, k_send.at[1], k_recv.at[1], (tm, s + 1))),
        (above, Send(kappa, first, kw, end, k_send.at[2], k_recv.at[2], (tm, s - 1))),
        (above, Send(rate, first, rw, end, k_send.at[3], k_recv.at[3], (tm, s - 1))),
        (even & below, Send(own, last, gb, upper, g_send.at[0], g_recv.at[0], (tm, s + 1))),
        (even & above, Send(own, first, gb, lower, g_send.at[1], g_recv.at[0], (tm + 1, s - 1))),
        (odd & later & below, Send(own, last, ga, upper, g_send.at[0], g_recv.at[2], (tm + 1, s + 1))),
        (odd & later & above, Send(own, first, ga, lower, g_send.at[1], g_recv.at[2], (tm + 2, s - 1))),
        (even, Send(own, tail, gb, main_odd, g_send.at[2], g_recv.at[1], (partner, s))),
        (odd & later, Send(own, tail, ga, main_odd, g_send.at[2], g_recv.at[3], (tm + 2, s))),
        (odd & later, Send(own, head, ga, main_even, g_send.at[3], g_recv.at[3], (tm + 1, s))),
    ]
    halves, fields = sends[:4], sends[4:]
    count = sum(condition.astype(jnp.int32) for condition, _ in targets)
    pl.semaphore_wait(barrier, count)
    for condition, transfer in sends:
        @pl.when(condition)
        def _(transfer=transfer):
            transfer.start()

    zeros = jnp.zeros((tiles, PAD, LANES), jnp.float32)
    for ref in (ga, gb, x_ref, ya, yb, z_ref, w_ref, cr, vo, vw, u1, u2):
        ref[:, pl.ds(0, PAD), :] = zeros
        ref[:, pl.ds(ref.shape[1] - PAD, PAD), :] = zeros
    rim = jnp.zeros((tiles, 2 * STEPS, LANES), jnp.float32)
    for ref in (cr, vo):
        ref[:, pl.ds(PAD, 2 * STEPS), :] = rim
        ref[:, pl.ds(wide - PAD - 2 * STEPS, 2 * STEPS), :] = rim
    blank = jnp.zeros((tiles, halo, LANES), jnp.float32)

    @pl.when(even & ~above)
    def _():
        ga[:, upper, :] = blank
        gb[:, upper, :] = blank

    @pl.when(odd & ~below)
    def _():
        ga[:, lower, :] = blank
        gb[:, lower, :] = blank

    @pl.when(~above)
    def _():
        kw[:, upper, :] = blank
        rw[:, upper, :] = blank

    @pl.when(~below)
    def _():
        kw[:, end, :] = blank
        rw[:, end, :] = blank

    k_local[1]()
    r_local[1]()

    @pl.when(above)
    def _():
        halves[0][1].wait_recv()
        halves[1][1].wait_recv()

    @pl.when(below)
    def _():
        halves[2][1].wait_recv()
        halves[3][1].wait_recv()

    def scaled(index, carry):
        part = pl.ds(pl.multiple_of(index * 32 + PAD, 8), 32)
        k = DIFFUSION * kw[:, part, :]
        kw[:, part, :] = k
        aw[:, part, :] = (1.0 + rw[:, part, :]) - 4.0 * k
        return carry

    lax.fori_loop(0, (rows + 2 * halo) // 32, scaled, 0)

    def step(src, low, size, offset):
        lane = lax.broadcasted_iota(jnp.int32, (size, LANES), 1)
        at = pl.ds(pl.multiple_of(low + offset, 8), size)
        here = pl.ds(pl.multiple_of(low, 8), size)
        centres = [src[t, here, :] for t in range(tiles)]
        to_right = [pltpu.roll(centre, 1, 1) for centre in centres]
        to_left = [pltpu.roll(centre, LANES - 1, 1) for centre in centres]
        results = []
        for t, centre in enumerate(centres):
            before = to_right[t - 1] if t > 0 else 0.0
            after = to_left[t + 1] if t + 1 < tiles else 0.0
            left = jnp.where(lane == 0, before, to_right[t])
            right = jnp.where(lane == LANES - 1, after, to_left[t])
            beside = src[t, pl.ds(low - 1, size), :] + src[t, pl.ds(low + 1, size), :]
            total = beside + (left + right)
            own_part = centre * (aw[t, at, :] - rw[t, at, :] * (centre * centre))
            results.append(own_part + kw[t, at, :] * total)
        return results, centres

    block = block_of(wide - 2 * PAD)

    def sweep(src, dst):
        def body(index, carry):
            low = index * block + PAD
            results, _ = step(src, low, block, shift)
            for t, value in enumerate(results):
                dst[t, pl.ds(pl.multiple_of(low, 8), block), :] = value
            return carry

        lax.fori_loop(0, (wide - 2 * PAD) // block, body, 0)

    def march(src, scratch, dst, times):
        for turn in range(times):
            out = dst if (times - 1 - turn) % 2 == 0 else scratch
            sweep(src, out)
            src = out

    def defects(field, relaxed, out, weight):
        march(field, x_ref, relaxed, STEPS)
        sweep(relaxed, w_ref)
        march(w_ref, z_ref, x_ref, STEPS - 2)

        def body(index, carry):
            low = index * block + PAD
            here = pl.ds(pl.multiple_of(low, 8), block)
            results, _ = step(x_ref, low, block, shift)
            for t, fine in enumerate(results):
                coarse = coarse_scale * w_ref[t, here, :] - (coarse_scale - 1.0) * relaxed[t, here, :]
                out[t, here, :] = fine - weight * coarse
            return carry

        lax.fori_loop(0, (wide - 2 * PAD) // block, body, 0)

    @pl.when(later)
    def _():
        @pl.when(even)
        def _():
            g_local[1]()

        @pl.when(even & above)
        def _():
            fields[0][1].wait_recv()

        @pl.when(odd & below)
        def _():
            fields[1][1].wait_recv()

        @pl.when(odd)
        def _():
            fields[4][1].wait_recv()

        defects(gb, yb, db, jnp.where(p == 0, 0.0, 1.0))

    @pl.when(earlier)
    def _():
        @pl.when(even & above)
        def _():
            fields[2][1].wait_recv()

        @pl.when(odd & below)
        def _():
            fields[3][1].wait_recv()

        @pl.when(even)
        def _():
            fields[6][1].wait_recv()

        @pl.when(odd)
        def _():
            fields[5][1].wait_recv()

        defects(ga, ya, da, 1.0)

    base = PAD + 2 * STEPS

    def chunk(index):
        return pl.ds(pl.multiple_of(index * CHUNK + base, 8), CHUNK)

    def chain(index):
        part = chunk(index)
        return copy(ve.at[:, part], cr.at[:, part], c_send.at[index], c_recv.at[index], (tm + 2, s))

    def target(index, side):
        return pl.ds(pl.multiple_of(index * CHUNK + PAD + side * half, 8), CHUNK)

    def forward(index, src):
        return copy(
            src.at[:, chunk(index)], vw.at[:, target(index, b)], f_send.at[index], f_recv.at[index],
            (partner, s),
        )

    def hand_over(index):
        @pl.when(even & (index < kept))
        def _():
            forward(index, vo).start()
            vw[:, target(index, 0), :] = cr[:, chunk(index), :]

        @pl.when(odd & (index >= skipped))
        def _():
            forward(index, cr).start()
            vw[:, target(index, 1), :] = vo[:, chunk(index), :]

    def corrected(src, defect, out, index):
        here = chunk(index)
        results, centres = step(src, index * CHUNK + base, CHUNK, shift)
        for t, value in enumerate(results):
            image = coarse_scale * value - (coarse_scale - 1.0) * centres[t]
            out[t, here, :] = image + defect[t, here, :]

    @pl.when(p == 0)
    def _():
        def body(index, carry):
            part = chunk(index)
            ve[:, part, :] = db[:, part, :]
            chain(index).start()
            vo[:, part, :] = yb[:, part, :]
            cr[:, part, :] = gb[:, part, :]
            hand_over(index)
            return carry

        lax.fori_loop(0, chunks, body, 0)

    @pl.when(earlier)
    def _():
        def body(index, carry):
            @pl.when(index < chunks)
            def _():
                chain(index).wait_recv()

            @pl.when((index >= 1) & (index <= chunks))
            def _():
                corrected(cr, da, vo, index - 1)

            @pl.when((index >= 2) & later)
            def _():
                corrected(vo, db, ve, index - 2)
                chain(index - 2).start()

            @pl.when((index >= 1) & (index <= chunks))
            def _():
                hand_over(index - 1)

            return carry

        lax.fori_loop(0, chunks + 2, body, 0)

    def collect(index, carry):
        forward(index + skipped * (1 - b), vo).wait_recv()
        return carry

    lax.fori_loop(0, kept, collect, 0)

    offset = halo - margin
    size = block_of(full - 2 * PAD)
    src = vw
    for turn in range(STEPS - 2):
        out = u1 if turn % 2 == 0 else u2

        def body(index, carry, src=src, out=out):
            low = index * size + PAD
            results, _ = step(src, low, size, offset)
            for t, value in enumerate(results):
                out[t, pl.ds(pl.multiple_of(low, 8), size), :] = value
            return carry

        lax.fori_loop(0, (full - 2 * PAD) // size, body, 0)
        src = out
    size_out = block_of(rows)

    def finish(index, carry):
        start = index * size_out
        low = start + PAD + margin
        out = pl.ds(pl.multiple_of(start, 8), size_out)
        results, _ = step(src, low, size_out, offset)
        for t, value in enumerate(results):
            lanes = pl.ds(t * LANES, LANES)
            f_out[0, out, lanes] = value
            c_out[0, out, lanes] = vw[t, pl.ds(pl.multiple_of(low, 8), size_out), :]
        return carry

    lax.fori_loop(0, rows // size_out, finish, 0)

    @pl.when(~later & even)
    def _():
        g_local[1]()

    @pl.when(~later)
    def _():
        @pl.when(even & above)
        def _():
            fields[0][1].wait_recv()

        @pl.when(odd & below)
        def _():
            fields[1][1].wait_recv()

        @pl.when(odd)
        def _():
            fields[4][1].wait_recv()

    for condition, transfer in sends:
        @pl.when(condition)
        def _(transfer=transfer):
            transfer.wait_send()

    @pl.when(later)
    def _():
        def body(index, carry):
            chain(index).wait_send()
            return carry

        lax.fori_loop(0, chunks, body, 0)

    def sent(index, carry):
        forward(index + skipped * b, vo).wait_send()
        return carry

    lax.fori_loop(0, kept, sent, 0)


def halo_of(points):
    needed = 2 * STEPS + max(points - 3, 0) + STEPS - 1
    return -(-needed // CHUNK) * CHUNK


def chained(points, strips, guess, kappa, rate):
    rows, width = kappa.shape
    tiles = width // LANES
    halo = halo_of(points)
    margin = halo - 2 * STEPS
    wide = rows // 2 + 2 * halo + 2 * PAD
    full = rows + 2 * margin + 2 * PAD
    chunks = (rows // 2 + 2 * margin) // CHUNK
    f32 = jnp.float32

    def held(height):
        return pltpu.VMEM((tiles, height, LANES), f32)

    part, whole, coefficient = held(wide), held(full), held(rows + 2 * halo + 2 * PAD)
    dma = pltpu.SemaphoreType.DMA
    vmem = pl.BlockSpec(memory_space=pltpu.VMEM)
    anywhere = pl.BlockSpec(memory_space=pl.ANY)
    return pl.pallas_call(
        functools.partial(kernel, points, strips),
        out_shape=[jax.ShapeDtypeStruct(guess.shape, f32)] * 2,
        in_specs=[anywhere] * 3,
        out_specs=[vmem] * 2,
        scratch_shapes=[coefficient] * 3 + [part] * 12 + [whole] * 3
        + [dma((3,))] + [dma((4,))] * 4 + [dma((chunks,))] * 4,
        compiler_params=pltpu.CompilerParams(
            collective_id=0, has_side_effects=True, vmem_limit_bytes=48 * 2**20
        ),
    )(guess, kappa, rate)


def extended(shard, sides, width):
    for axis, dim in sides:
        peers, length = (lax.axis_size(axis), shard.shape[dim])
        up = [(i, (i + 1) % peers) for i in range(peers - 1)]
        down = [(j, i) for i, j in up]
        last = lax.slice_in_dim(shard, length - width, length, axis=dim)
        initial = lax.slice_in_dim(shard, 0, width, axis=dim)
        before = lax.ppermute(last, axis, up)
        after = lax.ppermute(initial, axis, down)
        shard = jnp.concatenate([before, shard, after], axis=dim)
    return shard


def from_behind(value, axis, steps):
    count = lax.axis_size(axis)
    initial, last = (max(0, -steps), min(count, count - steps))
    return lax.ppermute(value, axis, [(source, source + steps) for source in range(initial, last)])


def advance_padded(padded, kappa, rate, scale):
    centre = padded[1:-1, 1:-1]
    laplace = (
        padded[2:, 1:-1] + padded[:-2, 1:-1] + padded[1:-1, 2:] + padded[1:-1, :-2] - 4.0 * centre
    )
    return centre + scale * (
        DIFFUSION * kappa * laplace + rate * (centre - centre * centre * centre)
    )


def deep_border(state, count):
    return extended(state, (("space", 0),), count)


def deep_step(wide, margin, widened, scale):
    rows = widened.shape[1] - 2 * STEPS
    height = wide.shape[0] - 2
    lower = STEPS - (margin - 1)
    kappa_rows = widened[0, lower : lower + height]
    rate_rows = widened[1, lower : lower + height]
    stepped = advance_padded(jnp.pad(wide, ((0, 0), (1, 1))), kappa_rows, rate_rows, scale)
    strip = lax.axis_index("space")
    total = rows * lax.axis_size("space")
    global_rows = strip * rows - (margin - 1) + lax.broadcasted_iota(jnp.int32, stepped.shape, 0)
    inside = (global_rows >= 0) & (global_rows < total)
    return jnp.where(inside, stepped, jnp.zeros_like(stepped))


def deep_march(wide, margin, widened, count):
    for repeat in range(count):
        wide = deep_step(wide, margin, widened, 1.0)
        margin = margin - 1
    return wide


def forward(state):
    return from_behind(state, "tm", 1)


def local(guess, kappa, rate):
    position = lax.axis_index("tm")
    member = position % GROUP
    coarse_scale = float(STEPS)
    state = guess[0]
    incoming = forward(state)
    widened = extended(jnp.stack([kappa, rate]), (("space", 1),), STEPS)
    marched = deep_march(deep_border(incoming, STEPS), STEPS, widened, STEPS)
    relaxed = jnp.where(position == 0, state, marched)
    incoming = forward(relaxed)
    wide = deep_border(incoming, STEPS)
    rows = relaxed.shape[0]
    band = jnp.pad(wide[STEPS - 1 : STEPS + rows + 1], ((0, 0), (1, 1)))
    coarse_image = advance_padded(band, kappa, rate, coarse_scale)
    fine_image = deep_march(wide, STEPS, widened, STEPS)
    defect = jnp.where(position == 0, jnp.zeros_like(fine_image), fine_image - coarse_image)
    coarse = relaxed
    for sweep_number in range(SWEEPS):
        for turn in range(GROUP):
            arrived = from_behind(coarse, "tm", 1)
            framed = extended(arrived, (("space", 0),), 1)
            framed = jnp.pad(framed, ((0, 0), (1, 1)))
            updated = advance_padded(framed, kappa, rate, coarse_scale) + defect
            if turn + 1 < GROUP:
                active = member == turn + 1
            else:
                active = (member == 0) & (position >= GROUP)
            coarse = jnp.where(active, updated, coarse)
    last_fine = deep_march(deep_border(coarse, STEPS - 1), STEPS - 1, widened, STEPS - 1)
    return (coarse[None], last_fine[None])


def solution(mesh):
    points, strips = mesh.shape["tm"], mesh.shape["space"]

    def run(guess, kappa, rate):
        rows, width = kappa.shape
        settled = points <= GROUP * SWEEPS and points % 2 == 0 and points >= 4
        aligned = rows % 32 == 0 and width % LANES == 0 and (2 * STEPS) % 8 == 0
        if settled and aligned and halo_of(points) % 16 == 0 and 2 * halo_of(points) <= rows:
            return tuple(chained(points, strips, guess, kappa, rate))
        return local(guess, kappa, rate)

    return jax.shard_map(
        run,
        mesh=mesh,
        in_specs=(P("tm", "space", None), P("space", None), P("space", None)),
        out_specs=(P("tm", "space", None), P("tm", "space", None)),
        check_vma=False,
    )
```

time: 80 us -> 66.9 us (0.84)
  Pallas kernels: 73.5 us -> 60.4 us
    pallas_call x1, Pallas kernels: 73.5 us -> 60.4 us  [chained(): pl.pallas_call(functools.partial(kernel, points, strips), out_shape=[jax....]
where the time goes in v2:
time: 66.9 us; the launch traced here: 66.7 us
  Pallas kernels  60.4 us (90%)
  local copies, waits for them, and re-layouts  5.61 us (8%)
    pallas_call x1, Pallas kernels, chained(): pl.pallas_call(functools.partial(kernel, points, strips), out_shape=[jax....  60.4 us
    unnamed x8, local copies, waits for them, and re-layouts  5.61 us

profile of v2, /device:TPU:27, one launch (start us, length us, event | category | flops | bytes accessed | tf_op | source)
XLA Modules:
  0.0 66.7 jit_solution(10325230460697720108)
XLA Ops:
  0.6 0.0 copy-start
  0.6 1.2 %copy-done = f32[1,256,1024]{2,1,0:T(8,128)S(1)} copy-done((f32[1,256,1024]{2,1,0:T(8,128)S(1)}, f32[1,256,1024]{2,1,0:T(8,128)}, u32[]{:S(2)}) %copy-start) | copy-done | bytes 1048600
  1.9 0.0 copy-start.1
  1.9 1.2 %copy-done.1 = f32[256,1024]{1,0:T(8,128)S(1)} copy-done((f32[256,1024]{1,0:T(8,128)S(1)}, f32[256,1024]{1,0:T(8,128)}, u32[]{:S(2)}) %copy-start.1) | copy-done | bytes 1048600
  3.1 0.0 copy-start.2
  3.1 1.2 %copy-done.2 = f32[256,1024]{1,0:T(8,128)S(1)} copy-done((f32[256,1024]{1,0:T(8,128)S(1)}, f32[256,1024]{1,0:T(8,128)}, u32[]{:S(2)}) %copy-start.2) | copy-done | bytes 1048600
  4.3 60.4 %shard_map.50 = (f32[1,256,1024]{2,1,0:T(8,128)S(1)}, f32[1,256,1024]{2,1,0:T(8,128)S(1)}) custom-call(f32[1,256,1024]{2,1,0:T(8,128)S(1)} %copy-done, f32[256,1024]{1,0:T(8,128)S(1)} %copy-done.1, f32[256,1024]{1,0:T(8,128)S(1)} %copy-done.2), custom_call_target="tpu_custom_call" | custom-call | tf_op jit(solution)/shard_map/pallas_call | solution.py:461
  64.7 1.0 %copy.7 = f32[1,256,1024]{2,1,0:T(8,128)} copy(f32[1,256,1024]{2,1,0:T(8,128)S(1)} %get-tuple-element.4) | data formatting | bytes 2097152
  65.7 1.0 %copy.8 = f32[1,256,1024]{2,1,0:T(8,128)} copy(f32[1,256,1024]{2,1,0:T(8,128)S(1)} %get-tuple-element.5) | data formatting | bytes 2097152
Async XLA Ops:
  0.6 1.2 %copy-start = (f32[1,256,1024]{2,1,0:T(8,128)S(1)}, f32[1,256,1024]{2,1,0:T(8,128)}, u32[]{:S(2)}) copy-start(f32[1,256,1024]{2,1,0:T(8,128)} %guess.1) | copy-start | bytes 3145732
  1.9 1.2 %copy-start.1 = (f32[256,1024]{1,0:T(8,128)S(1)}, f32[256,1024]{1,0:T(8,128)}, u32[]{:S(2)}) copy-start(f32[256,1024]{1,0:T(8,128)} %kappa.1) | copy-start | bytes 3145732
  3.1 1.2 %copy-start.2 = (f32[256,1024]{1,0:T(8,128)S(1)}, f32[256,1024]{1,0:T(8,128)}, u32[]{:S(2)}) copy-start(f32[256,1024]{1,0:T(8,128)} %rate.1) | copy-start | bytes 3145732

commit v3 on v2

--- a/solution.py
+++ b/solution.py
@@ -19,7 +19,7 @@
 
 
 def block_of(rows):
-    return max(size for size in range(8, min(rows, 136) + 1, 8) if rows % size == 0)
+    return max(size for size in range(8, min(rows, 32) + 1, 8) if rows % size == 0)
 
 
 def kernel(
@@ -196,36 +196,46 @@
 
     lax.fori_loop(0, (rows + 2 * halo) // 32, scaled, 0)
 
-    def step(src, low, size, offset):
+    def step(src, low, size, offset, emit):
         lane = lax.broadcasted_iota(jnp.int32, (size, LANES), 1)
         at = pl.ds(pl.multiple_of(low + offset, 8), size)
         here = pl.ds(pl.multiple_of(low, 8), size)
-        centres = [src[t, here, :] for t in range(tiles)]
-        to_right = [pltpu.roll(centre, 1, 1) for centre in centres]
-        to_left = [pltpu.roll(centre, LANES - 1, 1) for centre in centres]
-        results = []
-        for t, centre in enumerate(centres):
-            before = to_right[t - 1] if t > 0 else 0.0
-            after = to_left[t + 1] if t + 1 < tiles else 0.0
-            left = jnp.where(lane == 0, before, to_right[t])
-            right = jnp.where(lane == LANES - 1, after, to_left[t])
+        centre = src[0, here, :]
+        before = after = 0.0
+        to_left = pltpu.roll(centre, LANES - 1, 1)
+        for t in range(tiles):
+            to_right = pltpu.roll(centre, 1, 1)
+            if t + 1 < tiles:
+                following = src[t + 1, here, :]
+                after = pltpu.roll(following, LANES - 1, 1)
+            else:
+                following, after = None, 0.0
+            left = jnp.where(lane == 0, before, to_right)
+            right = jnp.where(lane == LANES - 1, after, to_left)
             beside = src[t, pl.ds(low - 1, size), :] + src[t, pl.ds(low + 1, size), :]
             total = beside + (left + right)
             own_part = centre * (aw[t, at, :] - rw[t, at, :] * (centre * centre))
-            results.append(own_part + kw[t, at, :] * total)
-        return results, centres
-
-    block = block_of(wide - 2 * PAD)
-
-    def sweep(src, dst):
+            emit(t, own_part + kw[t, at, :] * total, centre)
+            before, centre, to_left = to_right, following, after
+
+    def over(start, stop, act):
+        size = block_of(stop - start)
+        count = (stop - start) // size
+
         def body(index, carry):
-            low = index * block + PAD
-            results, _ = step(src, low, block, shift)
-            for t, value in enumerate(results):
-                dst[t, pl.ds(pl.multiple_of(low, 8), block), :] = value
+            act(index * size + start, size)
             return carry
 
-        lax.fori_loop(0, (wide - 2 * PAD) // block, body, 0)
+        lax.fori_loop(0, count, body, 0, unroll=True)
+
+    def sweep(src, dst, start=PAD, stop=wide - PAD, offset=shift):
+        def act(low, size):
+            def emit(t, value, centre):
+                dst[t, pl.ds(pl.multiple_of(low, 8), size), :] = value
+
+            step(src, low, size, offset, emit)
+
+        over(start, stop, act)
 
     def march(src, scratch, dst, times):
         for turn in range(times):
@@ -238,16 +248,16 @@
         sweep(relaxed, w_ref)
         march(w_ref, z_ref, x_ref, STEPS - 2)
 
-        def body(index, carry):
-            low = index * block + PAD
-            here = pl.ds(pl.multiple_of(low, 8), block)
-            results, _ = step(x_ref, low, block, shift)
-            for t, fine in enumerate(results):
+        def act(low, size):
+            here = pl.ds(pl.multiple_of(low, 8), size)
+
+            def emit(t, fine, centre):
                 coarse = coarse_scale * w_ref[t, here, :] - (coarse_scale - 1.0) * relaxed[t, here, :]
                 out[t, here, :] = fine - weight * coarse
-            return carry
-
-        lax.fori_loop(0, (wide - 2 * PAD) // block, body, 0)
+
+            step(x_ref, low, size, shift, emit)
+
+        over(PAD, wide - PAD, act)
 
     @pl.when(later)
     def _():
@@ -320,10 +330,12 @@
 
     def corrected(src, defect, out, index):
         here = chunk(index)
-        results, centres = step(src, index * CHUNK + base, CHUNK, shift)
-        for t, value in enumerate(results):
-            image = coarse_scale * value - (coarse_scale - 1.0) * centres[t]
+
+        def emit(t, value, centre):
+            image = coarse_scale * value - (coarse_scale - 1.0) * centre
             out[t, here, :] = image + defect[t, here, :]
+
+        step(src, index * CHUNK + base, CHUNK, shift, emit)
 
     @pl.when(p == 0)
     def _():
@@ -369,34 +381,23 @@
     lax.fori_loop(0, kept, collect, 0)
 
     offset = halo - margin
-    size = block_of(full - 2 * PAD)
     src = vw
     for turn in range(STEPS - 2):
         out = u1 if turn % 2 == 0 else u2
-
-        def body(index, carry, src=src, out=out):
-            low = index * size + PAD
-            results, _ = step(src, low, size, offset)
-            for t, value in enumerate(results):
-                out[t, pl.ds(pl.multiple_of(low, 8), size), :] = value
-            return carry
-
-        lax.fori_loop(0, (full - 2 * PAD) // size, body, 0)
+        sweep(src, out, PAD, full - PAD, offset)
         src = out
-    size_out = block_of(rows)
-
-    def finish(index, carry):
-        start = index * size_out
-        low = start + PAD + margin
-        out = pl.ds(pl.multiple_of(start, 8), size_out)
-        results, _ = step(src, low, size_out, offset)
-        for t, value in enumerate(results):
+
+    def finish(low, size):
+        out = pl.ds(pl.multiple_of(low - PAD - margin, 8), size)
+
+        def emit(t, value, centre):
             lanes = pl.ds(t * LANES, LANES)
             f_out[0, out, lanes] = value
-            c_out[0, out, lanes] = vw[t, pl.ds(pl.multiple_of(low, 8), size_out), :]
-        return carry
-
-    lax.fori_loop(0, rows // size_out, finish, 0)
+            c_out[0, out, lanes] = vw[t, pl.ds(pl.multiple_of(low, 8), size), :]
+
+        step(src, low, size, offset, emit)
+
+    over(PAD + margin, PAD + margin + rows, finish)
 
     @pl.when(~later & even)
     def _():
@@ -457,7 +458,7 @@
     part, whole, coefficient = held(wide), held(full), held(rows + 2 * halo + 2 * PAD)
     dma = pltpu.SemaphoreType.DMA
     vmem = pl.BlockSpec(memory_space=pltpu.VMEM)
-    anywhere = pl.BlockSpec(memory_space=pl.ANY)
+    anywhere = pl.BlockSpec(memory_space=pltpu.HBM)
     return pl.pallas_call(
         functools.partial(kernel, points, strips),
         out_shape=[jax.ShapeDtypeStruct(guess.shape, f32)] * 2,
@@ -466,7 +467,7 @@
         scratch_shapes=[coefficient] * 3 + [part] * 12 + [whole] * 3
         + [dma((3,))] + [dma((4,))] * 4 + [dma((chunks,))] * 4,
         compiler_params=pltpu.CompilerParams(
-            collective_id=0, has_side_effects=True, vmem_limit_bytes=48 * 2**20
+            collective_id=0, has_side_effects=True, vmem_limit_bytes=63 * 2**20
         ),
     )(guess, kappa, rate)
 

time: 66.9 us -> 64.3 us (0.961); the launches traced: 66.7 us -> 63.4 us
  local copies, waits for them, and re-layouts: 5.61 us -> 3.37 us
  Pallas kernels: 60.4 us -> 59.4 us
    unnamed x8 -> x4, local copies, waits for them, and re-layouts: 5.61 us -> 3.37 us
    pallas_call x1, Pallas kernels: 60.4 us -> 59.4 us  [chained(): pl.pallas_call(functools.partial(kernel, points, strips), out_shape=[jax....]
where the time goes in v3:
time: 64.3 us; the launch traced here: 63.4 us
  Pallas kernels  59.4 us (92%)
  local copies, waits for them, and re-layouts  3.37 us (5%)
  between operations  0.65 us (1%)
    pallas_call x1, Pallas kernels, chained(): pl.pallas_call(functools.partial(kernel, points, strips), out_shape=[jax....  59.4 us
    unnamed x4, local copies, waits for them, and re-layouts  3.37 us

profile of v3, /device:TPU:27, one launch (start us, length us, event | category | flops | bytes accessed | tf_op | source)
XLA Modules:
  0.0 63.4 jit_solution(7924397230560599452)
XLA Ops:
  0.6 59.4 %shard_map.50 = (f32[1,256,1024]{2,1,0:T(8,128)}, f32[1,256,1024]{2,1,0:T(8,128)}) custom-call(f32[1,256,1024]{2,1,0:T(8,128)} %guess.1, f32[256,1024]{1,0:T(8,128)} %kappa.1, f32[256,1024]{1,0:T(8,128)} %rate.1), custom_call_target="tpu_custom_call" | custom-call | tf_op jit(solution)/shard_map/pallas_call | solution.py:462
  60.0 0.0 copy-start
  60.0 2.4 %copy.7 = f32[1,256,1024]{2,1,0:T(8,128)} copy(f32[1,256,1024]{2,1,0:T(8,128)} %get-tuple-element.4) | data formatting | bytes 2097152
  62.4 0.0 copy-done
  62.4 1.0 %copy.8 = f32[1,256,1024]{2,1,0:T(8,128)} copy(f32[1,256,1024]{2,1,0:T(8,128)S(1)} %copy-done) | data formatting | bytes 2097152
Async XLA Ops:
  60.0 2.4 %copy-start = (f32[1,256,1024]{2,1,0:T(8,128)S(1)}, f32[1,256,1024]{2,1,0:T(8,128)}, u32[]{:S(2)}) copy-start(f32[1,256,1024]{2,1,0:T(8,128)} %get-tuple-element.5) | copy-start | bytes 3145732

commit v4 on v3

--- a/solution.py
+++ b/solution.py
@@ -14,6 +14,7 @@
 DIFFUSION = 0.05
 PAD = 8
 CHUNK = 8
+PIECES = 6
 LANES = 128
 MESH = pl.DeviceIdType.MESH
 
@@ -24,8 +25,9 @@
 
 def kernel(
     points, strips, guess, kappa, rate, c_out, f_out,
-    kw, rw, aw, ga, gb, x_ref, ya, yb, z_ref, w_ref, da, db, cr, vo, ve, vw, u1, u2,
+    kw, rw, aw, ga, gb, x_ref, ya, yb, z_ref, w_ref, da, db, cr, vo, ve, vw, u1, u2, st,
     local_sem, k_send, k_recv, g_send, g_recv, c_send, c_recv, f_send, f_recv,
+    t_send, t_recv, o_send, o_recv,
 ):
     rows, width = kappa.shape
     tiles = width // LANES
@@ -51,13 +53,13 @@
     targets = [
         (below, (tm, s + 1)), (above, (tm, s - 1)), (s >= 0, (partner, s)),
         (even & above, (tm + 1, s - 1)), (later, (tm + 2, s)),
-        (odd & later, (tm + 1, s)), (odd & later & below, (tm + 1, s + 1)),
+        (odd & later & below, (tm + 1, s + 1)),
         (odd & later & above, (tm + 2, s - 1)),
     ]
     sources = [
         (below, (tm, s + 1)), (above, (tm, s - 1)), (s >= 0, (partner, s)),
         (odd & below, (tm - 1, s + 1)), (earlier, (tm - 2, s)),
-        (even & earlier, (tm - 1, s)), (even & earlier & above, (tm - 1, s - 1)),
+        (even & earlier & above, (tm - 1, s - 1)),
         (odd & earlier & below, (tm - 2, s + 1)),
     ]
     barrier = pltpu.get_barrier_semaphore()
@@ -134,7 +136,16 @@
         (odd & later & above, Send(own, first, ga, lower, g_send.at[1], g_recv.at[2], (tm + 2, s - 1))),
         (even, Send(own, tail, gb, main_odd, g_send.at[2], g_recv.at[1], (partner, s))),
         (odd & later, Send(own, tail, ga, main_odd, g_send.at[2], g_recv.at[3], (tm + 2, s))),
-        (odd & later, Send(own, head, ga, main_even, g_send.at[3], g_recv.at[3], (tm + 1, s))),
+    ]
+    piece = main // PIECES
+    relays = [
+        Send(own, (i * piece, piece), st, pl.ds(i * piece, piece), t_send.at[i], t_recv.at[i], (partner, s))
+        for i in range(PIECES)
+    ]
+    onward = [
+        copy(st.at[:, pl.ds(i * piece, piece)], ga.at[:, pl.ds(PAD + halo + i * piece, piece)],
+             o_send.at[i], o_recv.at[i], (tm + 2, s))
+        for i in range(PIECES)
     ]
     halves, fields = sends[:4], sends[4:]
     count = sum(condition.astype(jnp.int32) for condition, _ in targets)
@@ -143,6 +154,11 @@
         @pl.when(condition)
         def _(transfer=transfer):
             transfer.start()
+
+    @pl.when(odd & later)
+    def _():
+        for relay in relays:
+            relay.start()
 
     zeros = jnp.zeros((tiles, PAD, LANES), jnp.float32)
     for ref in (ga, gb, x_ref, ya, yb, z_ref, w_ref, cr, vo, vw, u1, u2):
@@ -173,6 +189,12 @@
     def _():
         kw[:, end, :] = blank
         rw[:, end, :] = blank
+
+    @pl.when(even & later)
+    def _():
+        for relay, step_on in zip(relays, onward):
+            relay.wait_recv()
+            step_on.start()
 
     k_local[1]()
     r_local[1]()
@@ -291,7 +313,8 @@
 
         @pl.when(even)
         def _():
-            fields[6][1].wait_recv()
+            for step_on in onward:
+                step_on.wait_recv()
 
         @pl.when(odd)
         def _():
@@ -429,6 +452,16 @@
             return carry
 
         lax.fori_loop(0, chunks, body, 0)
+
+    @pl.when(odd & later)
+    def _():
+        for relay in relays:
+            relay.wait_send()
+
+    @pl.when(even & later)
+    def _():
+        for step_on in onward:
+            step_on.wait_send()
 
     def sent(index, carry):
         forward(index + skipped * b, vo).wait_send()
@@ -464,8 +497,8 @@
         out_shape=[jax.ShapeDtypeStruct(guess.shape, f32)] * 2,
         in_specs=[anywhere] * 3,
         out_specs=[vmem] * 2,
-        scratch_shapes=[coefficient] * 3 + [part] * 12 + [whole] * 3
-        + [dma((3,))] + [dma((4,))] * 4 + [dma((chunks,))] * 4,
+        scratch_shapes=[coefficient] * 3 + [part] * 12 + [whole] * 3 + [held(rows // 2 + halo)]
+        + [dma((3,))] + [dma((4,))] * 4 + [dma((chunks,))] * 4 + [dma((PIECES,))] * 4,
         compiler_params=pltpu.CompilerParams(
             collective_id=0, has_side_effects=True, vmem_limit_bytes=63 * 2**20
         ),
@@ -569,7 +602,7 @@
         rows, width = kappa.shape
         settled = points <= GROUP * SWEEPS and points % 2 == 0 and points >= 4
         aligned = rows % 32 == 0 and width % LANES == 0 and (2 * STEPS) % 8 == 0
-        if settled and aligned and halo_of(points) % 16 == 0 and 2 * halo_of(points) <= rows:
+        if settled and aligned and halo_of(points) % 16 == 0 and (rows // 2 + halo_of(points)) % (8 * PIECES) == 0 and 2 * halo_of(points) <= rows:
             return tuple(chained(points, strips, guess, kappa, rate))
         return local(guess, kappa, rate)
 

time: 64.3 us -> 54.1 us (0.84)
  Pallas kernels: 59.4 us -> 49.2 us
    pallas_call x1, Pallas kernels: 59.4 us -> 49.2 us  [chained(): pl.pallas_call(functools.partial(kernel, points, strips), out_shape=[jax....]
where the time goes in v4:
time: 54.1 us; the launch traced here: 53.2 us
  Pallas kernels  49.2 us (91%)
  local copies, waits for them, and re-layouts  3.37 us (6%)
  between operations  0.65 us (1%)
    pallas_call x1, Pallas kernels, chained(): pl.pallas_call(functools.partial(kernel, points, strips), out_shape=[jax....  49.2 us
    unnamed x4, local copies, waits for them, and re-layouts  3.37 us

profile of v4, /device:TPU:27, one launch (start us, length us, event | category | flops | bytes accessed | tf_op | source)
XLA Modules:
  0.0 53.2 jit_solution(13955497600835787288)
XLA Ops:
  0.6 49.2 %shard_map.50 = (f32[1,256,1024]{2,1,0:T(8,128)}, f32[1,256,1024]{2,1,0:T(8,128)}) custom-call(f32[1,256,1024]{2,1,0:T(8,128)} %guess.1, f32[256,1024]{1,0:T(8,128)} %kappa.1, f32[256,1024]{1,0:T(8,128)} %rate.1), custom_call_target="tpu_custom_call" | custom-call | tf_op jit(solution)/shard_map/pallas_call | solution.py:495
  49.8 0.0 copy-start
  49.8 2.4 %copy.7 = f32[1,256,1024]{2,1,0:T(8,128)} copy(f32[1,256,1024]{2,1,0:T(8,128)} %get-tuple-element.4) | data formatting | bytes 2097152
  52.2 0.0 copy-done
  52.2 1.0 %copy.8 = f32[1,256,1024]{2,1,0:T(8,128)} copy(f32[1,256,1024]{2,1,0:T(8,128)S(1)} %copy-done) | data formatting | bytes 2097152
Async XLA Ops:
  49.8 2.4 %copy-start = (f32[1,256,1024]{2,1,0:T(8,128)S(1)}, f32[1,256,1024]{2,1,0:T(8,128)}, u32[]{:S(2)}) copy-start(f32[1,256,1024]{2,1,0:T(8,128)} %get-tuple-element.5) | copy-start | bytes 3145732

commit v5 on v4

--- a/solution.py
+++ b/solution.py
@@ -14,7 +14,7 @@
 DIFFUSION = 0.05
 PAD = 8
 CHUNK = 8
-PIECES = 6
+PIECES = 9
 LANES = 128
 MESH = pl.DeviceIdType.MESH
 
@@ -69,10 +69,14 @@
             pl.semaphore_signal(barrier, inc=1, device_id=device, device_id_type=MESH)
 
     main = half + halo
+    cut = PAD + (wide - 2 * PAD) // 16 * 8
+    early = cut + 8 - PAD
+    early_odd, late_odd = pl.ds(PAD, early), pl.ds(PAD + early, main - early)
     first, last = (0, halo), (rows - halo, halo)
-    head, tail = (0, main), (rows - main, main)
+    head = (0, main)
+    tails = (rows - main, early), (rows - main + early, main - early)
     upper, lower = pl.ds(PAD, halo), pl.ds(PAD + main, halo)
-    main_even, main_odd = pl.ds(PAD + halo, main), pl.ds(PAD, main)
+    main_even = pl.ds(PAD + halo, main)
     end = pl.ds(PAD + halo + rows, halo)
     middle = pl.ds(PAD + halo, rows)
     own = guess.at[0]
@@ -134,8 +138,10 @@
         (even & above, Send(own, first, gb, lower, g_send.at[1], g_recv.at[0], (tm + 1, s - 1))),
         (odd & later & below, Send(own, last, ga, upper, g_send.at[0], g_recv.at[2], (tm + 1, s + 1))),
         (odd & later & above, Send(own, first, ga, lower, g_send.at[1], g_recv.at[2], (tm + 2, s - 1))),
-        (even, Send(own, tail, gb, main_odd, g_send.at[2], g_recv.at[1], (partner, s))),
-        (odd & later, Send(own, tail, ga, main_odd, g_send.at[2], g_recv.at[3], (tm + 2, s))),
+        (even, Send(own, tails[0], gb, early_odd, g_send.at[2], g_recv.at[1], (partner, s))),
+        (odd & later, Send(own, tails[0], ga, early_odd, g_send.at[2], g_recv.at[3], (tm + 2, s))),
+        (even, Send(own, tails[1], gb, late_odd, g_send.at[3], g_recv.at[4], (partner, s))),
+        (odd & later, Send(own, tails[1], ga, late_odd, g_send.at[3], g_recv.at[5], (tm + 2, s))),
     ]
     piece = main // PIECES
     relays = [
@@ -189,12 +195,6 @@
     def _():
         kw[:, end, :] = blank
         rw[:, end, :] = blank
-
-    @pl.when(even & later)
-    def _():
-        for relay, step_on in zip(relays, onward):
-            relay.wait_recv()
-            step_on.start()
 
     k_local[1]()
     r_local[1]()
@@ -259,16 +259,16 @@
 
         over(start, stop, act)
 
-    def march(src, scratch, dst, times):
+    def march(src, pair, dst, times, start, stop, keep):
         for turn in range(times):
-            out = dst if (times - 1 - turn) % 2 == 0 else scratch
-            sweep(src, out)
+            out = dst if turn == times - 1 else pair[turn % 2]
+            sweep(src, out, keep if turn == times - 1 else start, stop)
             src = out
 
-    def defects(field, relaxed, out, weight):
-        march(field, x_ref, relaxed, STEPS)
-        sweep(relaxed, w_ref)
-        march(w_ref, z_ref, x_ref, STEPS - 2)
+    def defects(field, relaxed, out, weight, start, stop, keep):
+        march(field, (x_ref, z_ref), relaxed, STEPS, start, stop, keep)
+        sweep(relaxed, w_ref, start, stop)
+        march(w_ref, (z_ref, x_ref), x_ref, STEPS - 2, start, stop, start)
 
         def act(low, size):
             here = pl.ds(pl.multiple_of(low, 8), size)
@@ -279,48 +279,91 @@
 
             step(x_ref, low, size, shift, emit)
 
-        over(PAD, wide - PAD, act)
+        over(keep, stop, act)
+
+    early_rows = (PAD, cut, PAD)
+    late_rows = (cut - 4 * STEPS, wide - PAD, cut - 2 * STEPS)
+    needed = -(-(cut + 1 - PAD - halo) // piece)
+    weight = jnp.where(p == 0, 0.0, 1.0)
+
+    def relay_on(start, stop):
+        @pl.when(even & later)
+        def _():
+            for i in range(start, stop):
+                relays[i].wait_recv()
+                onward[i].start()
+
+    @pl.when(even)
+    def _():
+        g_local[1]()
+
+    @pl.when(even & above)
+    def _():
+        fields[0][1].wait_recv()
+
+    @pl.when(odd & below)
+    def _():
+        fields[1][1].wait_recv()
+
+    @pl.when(odd)
+    def _():
+        fields[4][1].wait_recv()
 
     @pl.when(later)
     def _():
+        defects(gb, yb, db, weight, *early_rows)
+
+    relay_on(0, needed - 1)
+
+    @pl.when(even & later)
+    def _():
+        defects(gb, yb, db, weight, *late_rows)
+
+    relay_on(needed - 1, PIECES - 2)
+
+    @pl.when(earlier)
+    def _():
+        @pl.when(even & above)
+        def _():
+            fields[2][1].wait_recv()
+
+        @pl.when(odd & below)
+        def _():
+            fields[3][1].wait_recv()
+
         @pl.when(even)
         def _():
-            g_local[1]()
-
-        @pl.when(even & above)
-        def _():
-            fields[0][1].wait_recv()
-
-        @pl.when(odd & below)
-        def _():
-            fields[1][1].wait_recv()
+            for step_on in onward[:needed]:
+                step_on.wait_recv()
 
         @pl.when(odd)
         def _():
-            fields[4][1].wait_recv()
-
-        defects(gb, yb, db, jnp.where(p == 0, 0.0, 1.0))
+            fields[5][1].wait_recv()
+
+        defects(ga, ya, da, 1.0, *early_rows)
+
+    relay_on(PIECES - 2, PIECES)
+
+    @pl.when(odd)
+    def _():
+        fields[6][1].wait_recv()
+
+    @pl.when(odd & later)
+    def _():
+        defects(gb, yb, db, weight, *late_rows)
 
     @pl.when(earlier)
     def _():
-        @pl.when(even & above)
-        def _():
-            fields[2][1].wait_recv()
-
-        @pl.when(odd & below)
-        def _():
-            fields[3][1].wait_recv()
-
         @pl.when(even)
         def _():
-            for step_on in onward:
+            for step_on in onward[needed:]:
                 step_on.wait_recv()
 
         @pl.when(odd)
         def _():
-            fields[5][1].wait_recv()
-
-        defects(ga, ya, da, 1.0)
+            fields[7][1].wait_recv()
+
+        defects(ga, ya, da, 1.0, *late_rows)
 
     base = PAD + 2 * STEPS
 
@@ -421,24 +464,6 @@
         step(src, low, size, offset, emit)
 
     over(PAD + margin, PAD + margin + rows, finish)
-
-    @pl.when(~later & even)
-    def _():
-        g_local[1]()
-
-    @pl.when(~later)
-    def _():
-        @pl.when(even & above)
-        def _():
-            fields[0][1].wait_recv()
-
-        @pl.when(odd & below)
-        def _():
-            fields[1][1].wait_recv()
-
-        @pl.when(odd)
-        def _():
-            fields[4][1].wait_recv()
 
     for condition, transfer in sends:
         @pl.when(condition)
@@ -498,7 +523,7 @@
         in_specs=[anywhere] * 3,
         out_specs=[vmem] * 2,
         scratch_shapes=[coefficient] * 3 + [part] * 12 + [whole] * 3 + [held(rows // 2 + halo)]
-        + [dma((3,))] + [dma((4,))] * 4 + [dma((chunks,))] * 4 + [dma((PIECES,))] * 4,
+        + [dma((3,))] + [dma((4,))] * 3 + [dma((6,))] + [dma((chunks,))] * 4 + [dma((PIECES,))] * 4,
         compiler_params=pltpu.CompilerParams(
             collective_id=0, has_side_effects=True, vmem_limit_bytes=63 * 2**20
         ),

time: 54.1 us -> 52.9 us (0.978)
  Pallas kernels: 49.2 us -> 48 us
    pallas_call x1, Pallas kernels: 49.2 us -> 48 us  [chained(): pl.pallas_call(functools.partial(kernel, points, strips), out_shape=[jax....]
where the time goes in v5:
time: 52.9 us; the launch traced here: 52 us
  Pallas kernels  48 us (91%)
  local copies, waits for them, and re-layouts  3.37 us (6%)
  between operations  0.65 us (1%)
    pallas_call x1, Pallas kernels, chained(): pl.pallas_call(functools.partial(kernel, points, strips), out_shape=[jax....  48 us
    unnamed x4, local copies, waits for them, and re-layouts  3.37 us

profile of v5, /device:TPU:27, one launch (start us, length us, event | category | flops | bytes accessed | tf_op | source)
XLA Modules:
  0.0 52.0 jit_solution(15648685573212820282)
XLA Ops:
  0.6 48.0 %shard_map.50 = (f32[1,256,1024]{2,1,0:T(8,128)}, f32[1,256,1024]{2,1,0:T(8,128)}) custom-call(f32[1,256,1024]{2,1,0:T(8,128)} %guess.1, f32[256,1024]{1,0:T(8,128)} %kappa.1, f32[256,1024]{1,0:T(8,128)} %rate.1), custom_call_target="tpu_custom_call" | custom-call | tf_op jit(solution)/shard_map/pallas_call | solution.py:520
  48.6 0.0 copy-start
  48.6 2.4 %copy.7 = f32[1,256,1024]{2,1,0:T(8,128)} copy(f32[1,256,1024]{2,1,0:T(8,128)} %get-tuple-element.4) | data formatting | bytes 2097152
  51.0 0.0 copy-done
  51.0 1.0 %copy.8 = f32[1,256,1024]{2,1,0:T(8,128)} copy(f32[1,256,1024]{2,1,0:T(8,128)S(1)} %copy-done) | data formatting | bytes 2097152
Async XLA Ops:
  48.6 2.4 %copy-start = (f32[1,256,1024]{2,1,0:T(8,128)S(1)}, f32[1,256,1024]{2,1,0:T(8,128)}, u32[]{:S(2)}) copy-start(f32[1,256,1024]{2,1,0:T(8,128)} %get-tuple-element.5) | copy-start | bytes 3145732

commit v6 on v5

--- a/solution.py
+++ b/solution.py
@@ -525,7 +525,7 @@
         scratch_shapes=[coefficient] * 3 + [part] * 12 + [whole] * 3 + [held(rows // 2 + halo)]
         + [dma((3,))] + [dma((4,))] * 3 + [dma((6,))] + [dma((chunks,))] * 4 + [dma((PIECES,))] * 4,
         compiler_params=pltpu.CompilerParams(
-            collective_id=0, has_side_effects=True, vmem_limit_bytes=63 * 2**20
+            collective_id=0, has_side_effects=True, vmem_limit_bytes=51 * 2**20
         ),
     )(guess, kappa, rate)
 

time: 52.9 us -> 50.1 us (0.947)
  local copies, waits for them, and re-layouts: 3.37 us -> 1.94 us
  Pallas kernels: 48 us -> 46.6 us
    unnamed x4 -> x2, local copies, waits for them, and re-layouts: 3.37 us -> 1.94 us
    pallas_call x1, Pallas kernels: 48 us -> 46.6 us  [chained(): pl.pallas_call(functools.partial(kernel, points, strips), out_shape=[jax....]
where the time goes in v6:
time: 50.1 us; the launch traced here: 49.2 us
  Pallas kernels  46.6 us (93%)
  local copies, waits for them, and re-layouts  1.94 us (4%)
  between operations  0.64 us (1%)
    pallas_call x1, Pallas kernels, chained(): pl.pallas_call(functools.partial(kernel, points, strips), out_shape=[jax....  46.6 us
    unnamed x2, local copies, waits for them, and re-layouts  1.94 us

profile of v6, /device:TPU:27, one launch (start us, length us, event | category | flops | bytes accessed | tf_op | source)
XLA Modules:
  0.0 49.2 jit_solution(3422804493931167023)
XLA Ops:
  0.6 46.6 %shard_map.50 = (f32[1,256,1024]{2,1,0:T(8,128)S(1)}, f32[1,256,1024]{2,1,0:T(8,128)S(1)}) custom-call(f32[1,256,1024]{2,1,0:T(8,128)} %guess.1, f32[256,1024]{1,0:T(8,128)} %kappa.1, f32[256,1024]{1,0:T(8,128)} %rate.1), custom_call_target="tpu_custom_call" | custom-call | tf_op jit(solution)/shard_map/pallas_call | solution.py:520
  47.3 1.0 %copy.7 = f32[1,256,1024]{2,1,0:T(8,128)} copy(f32[1,256,1024]{2,1,0:T(8,128)S(1)} %get-tuple-element.4) | data formatting | bytes 2097152
  48.2 1.0 %copy.8 = f32[1,256,1024]{2,1,0:T(8,128)} copy(f32[1,256,1024]{2,1,0:T(8,128)S(1)} %get-tuple-element.5) | data formatting | bytes 2097152
